TPU v7x, 32 devices: a whole 2x2x4 slice. The times are simulated.
32 devices in a mesh: grp: 2 (over x), ty: 4 (over y, core), tx: 4 (over z).
Axes of the slice: x: 2, y: 2, z: 4, core: 2. Of those that a mesh axis runs over, the one named last changes fastest.
Arguments:
- adjoint_state: float32 [2, 5, 50, 48, 1536], P('grp', None, None, 'tx', 'ty'), may hold values from -6 to 6
- land_mask: int32 [2, 48, 1536], P('grp', 'tx', 'ty'), may hold values 0 or 1
- diffusivity: float32 [2, 48, 1536], P('grp', 'tx', 'ty'), may hold values from 0.02 to 0.24
- mixing: float32 [2, 5, 50, 50], P('grp'), may hold values from -0.875 to 0.875
- nudging: float32 [48, 1536], P('tx', 'ty'), may hold values from 0.1 to 1
- nest_x: int32 [16], P(('ty', 'tx')), may hold values from 0 to 8
- nest_y: int32 [16], P(('ty', 'tx')), may hold values from 0 to 256
- obs_forcing: float32 [2, 16, 16, 16], P('grp', ('ty', 'tx')), may hold values from -6 to 6
- obs_cell: int32 [2, 16, 16, 16], P('grp', None, None, ('ty', 'tx')), may hold values from 0 to 1151999
- obs_count: int32 [2, 16, 16], P('grp', None, ('ty', 'tx')), may hold values from 0 to 16, as said below
Outputs:
- updated_state: float32 [2, 5, 50, 48, 1536], P('grp', None, None, 'tx', 'ty')
Inputs may be any that keep to these rules, and one draw needn't show every extreme that they name: `obs_count`: in every draw some destination tile of each grid receives 16 live slots from every source tile; which one is drawn.
All inputs are finite; a program needn't handle non-finite values. No bound on the sum of `land_mask` on one device may be relied on, other than what follows from the above.
Results may differ from a plain program's by a relative error of at most 0.0003.
Values sent between devices are 32-bit elements; how exact they have to be, the bound alone decides.
No kernel may reach another device: no remote copies, remote signals or barrier semaphores. Data moves between devices by JAX's collectives and lax.ppermute only.
A program may use at most 128 MiB of HBM per device.

v0:
```python
import functools

import jax
import jax.numpy as jnp
from jax import lax
from jax.experimental import pallas as pl
from jax.experimental.pallas import tpu as pltpu
from jax.sharding import PartitionSpec as P

LANE = 128
PAD = 56
DEPTH = 64
MIB = 1 << 20
HBM = pl.BlockSpec(memory_space=pltpu.HBM)
SMEM = pl.BlockSpec(memory_space=pltpu.SMEM)
VMEM = pl.BlockSpec(memory_space=pltpu.VMEM)
F32 = jnp.float32
COST = pl.CostEstimate(flops=10**10, bytes_accessed=10**8, transcendentals=0)


def lane_ids(shape):
    return lax.broadcasted_iota(jnp.int32, shape, len(shape) - 1)


def row_of(ref, x):
    return ref[x].astype(F32)


def chunk(c):
    return slice(c * LANE, (c + 1) * LANE)


def in_hbm(value):
    return pltpu.with_memory_space_constraint(value, pltpu.HBM)


def in_vmem(value):
    return pltpu.with_memory_space_constraint(value, pltpu.VMEM)


def x_edges_kernel(tx, state, mask, first, second, ahead, buf, mask_buf, sems):
    fields, _, cols = state.shape[:3]
    even = lax.rem(tx[0], 2) == 0
    ends = (jnp.where(even, cols - 1, 0), jnp.where(even, 0, cols - 1))
    copies = [pltpu.make_async_copy(mask, mask_buf, sems.at[2 * fields])]
    for n, x in enumerate(ends):
        for f in range(fields):
            copies.append(
                pltpu.make_async_copy(state.at[f, :, x], buf.at[n, f], sems.at[n * fields + f])
            )
    copies.append(pltpu.make_async_copy(state.at[0], ahead, sems.at[2 * fields + 1]))
    for copy in copies:
        copy.start()
    copies[0].wait()
    for n, (x, out) in enumerate(zip(ends, (first, second))):
        for f in range(fields):
            copies[1 + n * fields + f].wait()
            out[f] = buf[n, f] * row_of(mask_buf, x)[None]
    copies[-1].wait()


def x_edges(tx, state5, mask):
    fields, levels, cols, _, rows = state5.shape
    edge = (fields, levels, 1, rows)
    return pl.pallas_call(
        x_edges_kernel,
        in_specs=[SMEM, HBM, HBM],
        out_specs=[VMEM] * 3,
        out_shape=[pltpu.VMEM(edge, F32)] * 2 + [pltpu.VMEM(state5.shape[1:], F32)],
        scratch_shapes=[
            pltpu.VMEM((2,) + edge, F32),
            pltpu.VMEM(mask.shape, jnp.int32),
            pltpu.SemaphoreType.DMA((2 * fields + 2,)),
        ],
        compiler_params=pltpu.CompilerParams(vmem_limit_bytes=8 * MIB),
        cost_estimate=COST,
        name="x_edges",
    )(tx, in_hbm(state5), in_hbm(mask))


def x_halos_of(tx, first, second, f):
    one, two = first[f, :, 0, :], second[f, :, 0, :]
    even = lax.rem(tx[0], 2) == 0
    return jnp.where(even, two, one), jnp.where(even, one, two)


def spread_of(here, above, below, kappa, edge=None):
    rows = here.shape[1]
    lanes = lane_ids((here.shape[0], LANE))
    edge = 0.0 if edge is None else edge
    before = pltpu.roll(here, 1, 1)
    after = pltpu.roll(here, rows - 1, 1)
    before = jnp.concatenate([jnp.where(lanes == 0, edge, before[:, :LANE]), before[:, LANE:]], 1)
    after = jnp.concatenate(
        [after[:, :-LANE], jnp.where(lanes == LANE - 1, edge, after[:, -LANE:])], 1
    )
    return here + kappa * (above + below + before + after - 4.0 * here)


def halves(value):
    high = value.astype(jnp.bfloat16)
    return high, (value - high.astype(F32)).astype(jnp.bfloat16)


def deepened(value):
    return jnp.concatenate([value, jnp.zeros((DEPTH - value.shape[0], value.shape[1]), F32)], 0)


def fill_matrix(levels, mixing, square, matrix):
    square[:levels, :levels] = mixing
    value = square[...]
    high = value.astype(jnp.bfloat16).astype(F32)
    matrix[:DEPTH, :] = (high + pltpu.roll(high, DEPTH, 1)).astype(jnp.bfloat16)
    matrix[DEPTH:, :] = (value - high).astype(jnp.bfloat16)


def fill_stack(stack, part, value):
    high, low = halves(value)
    stack[:DEPTH, part] = high
    stack[DEPTH:, part] = low


def mix(matrix, stack):
    both = jnp.dot(matrix, stack, preferred_element_type=F32)
    return both[:DEPTH] + both[DEPTH:]


def fill_group(group):
    rows = group.shape[0] // 2
    ids = lax.broadcasted_iota(jnp.int32, group.shape, 0)
    ids = jnp.where(ids < rows, ids, ids - rows) // 3
    group[...] = jnp.where(ids == lane_ids(group.shape), 1.0, 0.0).astype(jnp.bfloat16)


def grouped(wide, group):
    return jnp.dot(wide, group, preferred_element_type=F32)


def aligned(index, size):
    return pl.ds(pl.multiple_of(index * size, size), size)


def packed(rows_of, cols):
    parts = []
    for x in range(cols):
        first, last = rows_of(x)
        lanes = lane_ids(first.shape)
        parts.append(jnp.where(lanes == 0, first, jnp.where(lanes == LANE - 1, last, 0.0)))
    shift = 2
    while len(parts) > 1:
        pairs = [parts[n : n + 2] for n in range(0, len(parts), 2)]
        parts = [p[0] + pltpu.roll(p[1], shift, 1) if len(p) == 2 else p[0] for p in pairs]
        shift *= 2
    return parts[0]


def fill_masked(levels, state, f, mask, masked):
    cols, _, rows = masked.shape
    chunks = rows // LANE
    step = cols * chunks
    for x in range(cols):
        row = row_of(mask, x)
        masked[x, PAD - 8 :, :] = jnp.zeros((8, rows), F32)
        for c in range(chunks):
            at = pl.ds(f * (levels * step) + x * chunks + c, levels, stride=step)
            masked[x, :levels, chunk(c)] = state[at, :] * row[:, chunk(c)]


TERMS = 11


def join_weights(bs, cols, kappa, nudging, weights):
    rows = weights.shape[1]
    ids = lane_ids((1, rows))
    for i, b in enumerate(bs):
        own = range(3 * b, 3 * b + 3)
        both = {x: nudging[x : x + 1, :] * kappa[x] for x in own}
        for n, x in enumerate(range(3 * b - 1, 3 * b + 4)):
            total = None
            for near in (x - 1, x + 1):
                if near in both:
                    total = both[near] if total is None else total + both[near]
            if x in both:
                total = total + (nudging[x : x + 1, :] - 4.0 * both[x])
            weights[i * TERMS + n : i * TERMS + n + 1, :] = total
        for n, x in enumerate(own):
            at = i * TERMS + 5 + n
            value = jnp.where(ids == rows - 1, 0.0, pltpu.roll(both[x], rows - 1, 1))
            weights[at : at + 1, :] = value
            value = jnp.where(ids == 0, 0.0, pltpu.roll(both[x], 1, 1))
            weights[at + 3 : at + 4, :] = value


def child_rows(f, bs, masked, weights, wide):
    cols, _, rows = masked.shape[1:]
    for i, b in enumerate(bs):

        def term(n, x):
            at = i * TERMS + n
            return weights[at : at + 1, :] * masked[f, x]

        total = None
        for n, x in enumerate(range(3 * b - 1, 3 * b + 4)):
            if 0 <= x < cols:
                total = term(n, x) if total is None else total + term(n, x)
        for side, shift in ((5, 1), (8, rows - 1)):
            value = term(side, 3 * b) + term(side + 1, 3 * b + 1) + term(side + 2, 3 * b + 2)
            total = total + pltpu.roll(value, shift, 1)
        at = aligned(f * len(bs) + i, DEPTH)
        wide[at, :rows], wide[at, rows:] = halves(deepened(total))


def parent_rows(f, bs, nest_x, nest_y, masked, kappa, stack):
    cols, _, rows = masked.shape[1:]
    back = lax.rem(rows - nest_y[0], rows)
    for i, b in enumerate(bs):
        x = nest_x[0] + b
        above = masked[f, jnp.maximum(x - 1, 0)]
        below = masked[f, jnp.minimum(x + 1, cols - 1)]
        if b == 0:
            above = jnp.where(x == 0, 0.0, above)
        if b == cols // 3 - 1:
            below = jnp.where(x == cols - 1, 0.0, below)
        value = spread_of(masked[f, x], above, below, kappa[x])
        value = deepened(pltpu.roll(value, back, 1)[:, :LANE])
        fill_stack(stack.at[f], chunk(i), value)


def mix_rows(bs, is_child, wide, group, stack, matrices, emit):
    fields = stack.shape[0]

    @pl.when(is_child[0] == 1)
    def _():
        value = grouped(wide[...], group[...])
        for f in range(fields):
            for i in range(len(bs)):
                at = (f * len(bs) + i) * DEPTH
                fill_stack(stack.at[f], chunk(i), value[at : at + DEPTH])

    for f in range(fields):
        emit(f, mix(matrices[f], stack[f]))


def row_scratch(bs, fields, rows):
    return [
        pltpu.VMEM((-(-len(bs) * TERMS // 8) * 8, rows), F32),
        pltpu.VMEM((fields * len(bs) * DEPTH, 2 * rows), jnp.bfloat16),
        pltpu.VMEM((fields, 2 * DEPTH, len(bs) * LANE), jnp.bfloat16),
        pltpu.VMEM((2 * rows, LANE), jnp.bfloat16),
    ]


ROOM = 18


def front_kernel(
    levels, bs, slots, is_child, state, mask, kappa, nudging, mixing, nest_x, nest_y, ahead, cells, *refs
):
    refs = list(refs)
    line = [refs.pop(0) for _ in range(len(refs) - ROOM)]
    front_steps(
        levels, bs, slots, line, is_child, state, mask, kappa, nudging, mixing, nest_x, nest_y, ahead,
        cells, *refs
    )


def front_steps(
    levels, bs, slots, line, is_child, state, mask, kappa, nudging, mixing, nest_x, nest_y, ahead,
    cells, masked_out, matrices, parcel, inner, places,
    buf, masked, mask_buf, kappa_buf, nudging_buf, mixing_buf, square, weights, wide, stack, group, sems, out_sems,
):
    fields, cols, _, rows = masked.shape
    chunks = rows // LANE
    step = cols * chunks
    size = levels * step

    def copy(f):
        at = pl.ds(f * size, size)
        return pltpu.make_async_copy(state.at[at], buf.at[at], sems.at[f])

    def copy_out(f):
        return pltpu.make_async_copy(masked.at[f], masked_out.at[f], out_sems.at[f])

    pairs = (
        (mask, mask_buf),
        (kappa, kappa_buf),
        (nudging, nudging_buf),
        (mixing, mixing_buf),
    )
    smalls = [
        pltpu.make_async_copy(source, target, sems.at[fields + n])
        for n, (source, target) in enumerate(pairs)
    ]
    for small in smalls:
        small.start()
    for f in range(1, fields):
        copy(f).start()
    square[...] = jnp.zeros_like(square)
    cell = cells[...]
    column, inside = cell // (cols * rows), lax.rem(cell, cols * rows)
    piece = (column // levels) * step + inside // LANE
    place = (piece * PAD + lax.rem(column, levels)) * LANE + lax.rem(inside, LANE)
    places[...] = place
    for small in smalls:
        small.wait()

    @pl.when(is_child[0] == 1)
    def _():
        fill_group(group)
        join_weights(bs, cols, kappa_buf, nudging_buf, weights)

    def field(f, total_edges, first=False):
        fill_matrix(levels, mixing_buf[f, :, 0, :], square, matrices.at[f])
        if first:
            fill_masked(levels, ahead, f, mask_buf, masked.at[f])
        else:
            copy(f).wait()
            fill_masked(levels, buf, f, mask_buf, masked.at[f])
        copy_out(f).start()
        own_edges = packed(
            lambda x: (masked[f, x, :, :LANE], masked[f, x, :, rows - LANE :]), cols
        )

        @pl.when(is_child[0] == 1)
        def _():
            child_rows(f, bs, masked, weights, wide)

        @pl.when(is_child[0] == 0)
        def _():
            parent_rows(f, bs, nest_x, nest_y, masked, kappa_buf, stack)

        return total_edges + pltpu.roll(own_edges, 2 * f * cols, 1)

    own_edges = field(0, jnp.zeros((PAD, LANE), F32), first=True)
    parcel[:PAD, :] = lax.fori_loop(1, fields, field, own_edges)
    parcel[PAD:, :] = jnp.zeros((parcel.shape[0] - PAD, LANE), F32)
    lane = 0
    for blocks in line:
        dests = blocks.shape[1]
        for start in range(0, blocks.shape[0], slots):
            at = PAD + lane // LANE * slots
            part = slice(lane % LANE, lane % LANE + dests)
            parcel[at : at + slots, part] = blocks[start : start + slots, :]
            lane += dests

    def emit(f, mixed):
        for i in range(len(bs)):
            at = pl.ds(f * levels * len(bs) + i, levels, stride=len(bs))
            inner[at, :] = mixed[:levels, chunk(i)]

    mix_rows(bs, is_child, wide, group, stack, matrices, emit)
    for f in range(fields):
        copy_out(f).wait()


def front(is_child, state2, mask, kappa, nudging, mixing, nests, line, ahead, cells, dims):
    fields, levels, cols, chunks = dims
    rows = chunks * LANE
    bs = tuple(range(1, cols // 3 - 1))
    arrays = (state2, mask, kappa, nudging, mixing)
    slots = cells.shape[1]
    height = -(-sum(blocks.size for blocks in line) // (LANE * slots)) * slots
    return pl.pallas_call(
        functools.partial(front_kernel, levels, bs, slots),
        in_specs=[SMEM] + [HBM] * 5 + [SMEM] * 2 + [VMEM] * (2 + len(line)),
        out_specs=[HBM] + [VMEM] * 4,
        out_shape=[
            pltpu.HBM((fields, cols, PAD, rows), F32),
            pltpu.VMEM((fields, 2 * DEPTH, 2 * DEPTH), jnp.bfloat16),
            pltpu.VMEM((PAD + height, LANE), F32),
            pltpu.VMEM((fields * levels * len(bs), LANE), F32),
            pltpu.VMEM(cells.shape, jnp.int32),
        ],
        scratch_shapes=[
            pltpu.VMEM(state2.shape, F32),
            pltpu.VMEM((fields, cols, PAD, rows), F32),
            pltpu.VMEM(mask.shape, jnp.int32),
            pltpu.VMEM(kappa.shape, F32),
            pltpu.VMEM(nudging.shape, F32),
            pltpu.VMEM(mixing.shape, F32),
            pltpu.VMEM((DEPTH, LANE), F32),
        ]
        + row_scratch(bs, fields, rows)
        + [pltpu.SemaphoreType.DMA((fields + 4,)), pltpu.SemaphoreType.DMA((fields,))],
        compiler_params=pltpu.CompilerParams(vmem_limit_bytes=24 * MIB),
        cost_estimate=COST,
        name="front",
    )(is_child, *map(in_hbm, arrays), *nests, in_vmem(ahead), cells, *line)


def base_kernel(
    levels, bs, is_child, nest_x, nest_y, masked_in, matrices, kappa, nudging, base,
    masked, weights, wide, stack, group, sems,
):
    fields, cols = masked.shape[:2]
    near = cols // 3
    reach = near + 2

    def child_copies(f):
        for n, x in enumerate((0, cols - near)):
            at = pl.ds(x, near)
            yield pltpu.make_async_copy(masked_in.at[f, at], masked.at[f, at], sems.at[f, n])

    def parent_copy(f):
        at = pl.ds(jnp.clip(nest_x[0] - 1, 0, cols - reach), reach)
        return pltpu.make_async_copy(masked_in.at[f, at], masked.at[f, at], sems.at[f, 0])

    @pl.when(is_child[0] == 1)
    def _():
        for f in range(fields):
            for copy in child_copies(f):
                copy.start()
        fill_group(group)
        join_weights(bs, cols, kappa, nudging, weights)

        def field(f, carry):
            for copy in child_copies(f):
                copy.wait()
            child_rows(f, bs, masked, weights, wide)
            return carry

        lax.fori_loop(0, fields, field, 0)

    @pl.when(is_child[0] == 0)
    def _():
        for f in range(fields):
            parent_copy(f).start()

        def field(f, carry):
            parent_copy(f).wait()
            parent_rows(f, bs, nest_x, nest_y, masked, kappa, stack)
            return carry

        lax.fori_loop(0, fields, field, 0)

    def emit(f, mixed):
        base[f, :, :] = mixed[:PAD, :]

    mix_rows(bs, is_child, wide, group, stack, matrices, emit)


def base_of(is_child, nests, masked, matrices, kappa, nudging, dims):
    fields, levels, cols, chunks = dims
    rows = chunks * LANE
    bs = (0, cols // 3 - 1)
    return pl.pallas_call(
        functools.partial(base_kernel, levels, bs),
        in_specs=[SMEM] * 3 + [HBM] + [VMEM] * 3,
        out_specs=VMEM,
        out_shape=pltpu.VMEM((fields, PAD, 2 * LANE), F32),
        scratch_shapes=[pltpu.VMEM(masked.shape, F32)]
        + row_scratch(bs, fields, rows)
        + [pltpu.SemaphoreType.DMA((fields, 2))],
        compiler_params=pltpu.CompilerParams(vmem_limit_bytes=16 * MIB),
        cost_estimate=COST,
        name="base",
    )(is_child, *nests, in_hbm(masked), matrices, kappa, nudging)


def merged(own, other, width):
    if 2 * width <= LANE:
        return own + pltpu.roll(other, width, 1)
    return jnp.concatenate([own, other], axis=0)


def repack_kernel(width, edges, parcel, arrived, out):
    if edges:
        out[:edges, :] = parcel[:edges, :]
    out[edges:, :] = merged(parcel[PAD:, :], arrived[PAD:, :], width)


def repack(parcel, arrived, width, edges):
    height = (parcel.shape[0] - PAD) * (1 if 2 * width <= LANE else 2)
    return pl.pallas_call(
        functools.partial(repack_kernel, width, edges),
        in_specs=[VMEM] * 2,
        out_specs=VMEM,
        out_shape=pltpu.VMEM((edges + height, LANE), F32),
        compiler_params=pltpu.CompilerParams(vmem_limit_bytes=4 * MIB),
        name="repack",
    )(parcel, arrived)


def y_halos(ty, peers, first, second):
    one, two = first[:PAD, :], second[:PAD, :]
    even = (lax.rem(ty[0], 2) == 0).astype(F32)
    odd = 1.0 - even
    before = (two * even + one * odd) * (ty[0] > 0).astype(F32)
    after = (one * even + two * odd) * (ty[0] < peers - 1).astype(F32)
    low = lax.rem(lane_ids((PAD, LANE)), 2) == 0
    return jnp.where(low, pltpu.roll(before, 1, 1), pltpu.roll(after, LANE - 1, 1))


def outer_kernel(
    levels, peers, is_child, tx, ty, state, matrices, base, kappa, nudging, x_first, x_second,
    first, second, nest_x, nest_y, out, ahead, sides, wide, stack, group, sem,
):
    fields = matrices.shape[0]
    cols, _, rows = kappa.shape
    blocks = cols // 3
    lanes = lane_ids((PAD, LANE))
    turned = lax.rem(lanes + 1, LANE)
    copy = pltpu.make_async_copy(state.at[pl.ds(0, ahead.shape[0])], ahead, sem)
    copy.start()
    sides[...] = jnp.zeros_like(sides)
    halo = y_halos(ty, peers, first, second)

    def weighted(row_of_x):
        one = packed(lambda x: (row_of_x(x)[:, :LANE], row_of_x(x)[:, rows - LANE :]), cols)
        total = one
        for f in range(1, fields):
            total = total + pltpu.roll(one, 2 * f * cols, 1)
        return halo * total

    def fill_fix(value):
        for f in range(fields):
            fill_stack(stack.at[f], chunk(2), deepened(value))

    @pl.when(is_child[0] == 1)
    def _():
        fill_group(group)
        for f in range(fields):
            for n, side in enumerate(x_halos_of(tx, x_first, x_second, f)):
                x = (0, cols - 1)[n]
                at = (f * 2 + n) * DEPTH
                sides[at : at + levels, :] = side * (nudging[x : x + 1, :] * kappa[x])
        wide[:, :rows], wide[:, rows:] = halves(sides[...])
        value = grouped(wide[...], group[...])
        for f in range(fields):
            for n in range(2):
                at = (f * 2 + n) * DEPTH
                fill_stack(stack.at[f], chunk(n), value[at : at + DEPTH])
        part = weighted(lambda x: nudging[x : x + 1, :] * kappa[x])
        fill_fix(part + pltpu.roll(part, LANE - 2, 1) + pltpu.roll(part, LANE - 4, 1))

    @pl.when(is_child[0] == 0)
    def _():
        back = lax.rem(rows - nest_y[0], rows)
        reached = (nest_x[0] == 0, nest_x[0] + blocks == cols)
        for f in range(fields):
            for n, side in enumerate(x_halos_of(tx, x_first, x_second, f)):
                at = (f * 2 + n) * DEPTH
                weight = kappa[(0, cols - 1)[n]] * reached[n].astype(F32)
                sides[at : at + levels, :] = side * weight
                value = pltpu.roll(sides[at : at + DEPTH, :], back, 1)[:, :LANE]
                fill_stack(stack.at[f], chunk(n), value)
        starts = (nest_y[0] == 0).astype(F32)
        finals = (nest_y[0] == rows - LANE).astype(F32)
        part = weighted(lambda x: kappa[x])
        part = part * jnp.where(lax.rem(lanes, 2) == 0, starts, finals)
        value = jnp.zeros((PAD, LANE), F32)
        for b in range(blocks):
            shift = lax.rem(LANE + 4 * b - 2 * nest_x[0], LANE)
            here = lax.rem(turned, 2 * cols) // 2 == 3 * b
            value = jnp.where(here, pltpu.roll(part, shift, 1), value)
        fill_fix(value)

    fixes = jnp.zeros((PAD, LANE), F32)
    for f in range(fields):
        mixed = mix(matrices[f], stack[f])
        for n in range(2):
            at = pl.ds(f * (2 * levels) + n, levels, stride=2)
            out[at, :] = base[f, :levels, chunk(n)] + mixed[:levels, chunk(n)]
        fixes = jnp.where(turned // (2 * cols) == f, mixed[:PAD, chunk(2)], fixes)
    out[out.shape[0] - PAD :, :] = fixes
    copy.wait()


def outer(
    is_child, tx, ty, state2, matrices, base, kappa, nudging, x_halos, firsts, nests, dims, peers
):
    fields, levels, cols, chunks = dims
    rows = chunks * LANE
    height = -(-fields * 2 * levels // 8) * 8 + PAD
    return pl.pallas_call(
        functools.partial(outer_kernel, levels, peers),
        in_specs=[SMEM] * 3 + [HBM] + [VMEM] * 8 + [SMEM] * 2,
        out_specs=[VMEM] * 2,
        out_shape=[
            pltpu.VMEM((height, LANE), F32),
            pltpu.VMEM((state2.shape[0] // fields, LANE), F32),
        ],
        scratch_shapes=[
            pltpu.VMEM((fields * 2 * DEPTH, rows), F32),
            pltpu.VMEM((fields * 2 * DEPTH, 2 * rows), jnp.bfloat16),
            pltpu.VMEM((fields, 2 * DEPTH, 3 * LANE), jnp.bfloat16),
            pltpu.VMEM((2 * rows, LANE), jnp.bfloat16),
            pltpu.SemaphoreType.DMA,
        ],
        compiler_params=pltpu.CompilerParams(vmem_limit_bytes=12 * MIB),
        name="outer",
    )(is_child, tx, ty, in_hbm(state2), matrices, base, kappa, nudging, *x_halos, *firsts, *nests)


def tile_kernel(
    levels, peers, tx, ty, state, mask, matrices, kappa, x_first, x_second, first, second, ahead,
    out, buf, masked, sides, halo, stack, sems,
):
    cols, _, rows = masked.shape
    chunks = rows // LANE
    size = levels * cols * chunks
    fields = state.shape[0] // size

    def copy(f):
        at = pl.ds(f * size, size)
        return pltpu.make_async_copy(state.at[at], buf.at[at], sems.at[f])

    for f in range(1, fields):
        copy(f).start()
    sides[...] = jnp.zeros_like(sides)
    halo[...] = y_halos(ty, peers, first, second)
    pair = 2

    def field(f, carry, leading=False):
        if leading:
            fill_masked(levels, ahead, f, mask, masked)
        else:
            copy(f).wait()
            fill_masked(levels, buf, f, mask, masked)
        for n, side in enumerate(x_halos_of(tx, x_first, x_second, f)):
            sides[n, :levels, :] = side
        for x0 in range(0, cols, pair):
            for x in range(x0, x0 + pair):
                above = masked[x - 1] if x > 0 else sides[0]
                below = masked[x + 1] if x < cols - 1 else sides[1]
                shift = lax.rem(LANE - 2 * (f * cols + x), LANE)
                edge = pltpu.roll(halo[...], lax.rem(LANE + shift, LANE), 1)
                value = spread_of(masked[x], above, below, kappa[x], edge)
                part = slice((x - x0) * rows, (x - x0 + 1) * rows)
                fill_stack(stack, part, deepened(value))
            mixed = mix(matrices[f], stack[...])
            for n in range(pair * chunks):
                out[aligned((f * cols + x0) * chunks + n, PAD), :] = mixed[:PAD, chunk(n)]
        return carry

    field(0, 0, leading=True)
    lax.fori_loop(1, fields, field, 0)


def tile_of(tx, ty, state2, mask, matrices, kappa, x_halos, firsts, ahead, dims, peers):
    fields, levels, cols, chunks = dims
    rows = chunks * LANE
    return pl.pallas_call(
        functools.partial(tile_kernel, levels, peers),
        in_specs=[SMEM] * 2 + [HBM] + [VMEM] * 8,
        out_specs=VMEM,
        out_shape=pltpu.VMEM((fields * cols * chunks * PAD, LANE), F32),
        scratch_shapes=[
            pltpu.VMEM(state2.shape, F32),
            pltpu.VMEM((cols, PAD, rows), F32),
            pltpu.VMEM((2, PAD, rows), F32),
            pltpu.VMEM((PAD, LANE), F32),
            pltpu.VMEM((2 * DEPTH, 2 * rows), jnp.bfloat16),
            pltpu.SemaphoreType.DMA((fields,)),
        ],
        compiler_params=pltpu.CompilerParams(vmem_limit_bytes=16 * MIB),
        cost_estimate=COST,
        name="tile",
    )(tx, ty, in_hbm(state2), mask, matrices, kappa, *x_halos, *firsts, in_vmem(ahead))


def observe_kernel(dests, across, row, column, counts, places, mine, theirs, _, tile):
    lanes = lane_ids((1, LANE))
    slots = places.shape[1]
    ty, tx = row[0], column[0]
    me = ty * across + tx
    half = (mine.shape[0] - PAD) // slots * (LANE // dests)

    def source(turn, ref, g, carry):
        origin = (lax.div(g, across) ^ turn ^ ty) * across + (lax.rem(g, across) ^ tx)
        lane_in = lax.rem(g, LANE // dests) * dests + me
        block = PAD + lax.div(g, LANE // dests) * slots
        count = counts[0, origin]
        for k in range(0, slots, 2):
            ats, adds = [], []
            for m in range(k, k + 2):
                place = places[origin, m]
                lane = place & (LANE - 1)
                value = pltpu.roll(ref[pl.ds(block + m, 1), :], (lane - lane_in) & (LANE - 1), 1)
                ats.append(place >> 7)
                adds.append(jnp.where(lanes == jnp.where(m < count, lane, LANE), value, 0.0))
            olds = [tile[pl.ds(at, 1), :] for at in ats]
            also = jnp.where(ats[0] == ats[1], adds[0], 0.0)
            tile[pl.ds(ats[0], 1), :] = olds[0] + adds[0]
            tile[pl.ds(ats[1], 1), :] = olds[1] + adds[1] + also
        return carry

    lax.fori_loop(0, half, functools.partial(source, 0, mine), 0)
    lax.fori_loop(0, half, functools.partial(source, 3, theirs), 0)


def observe(row, column, places, counts, seen, tile, dests, across):
    return pl.pallas_call(
        functools.partial(observe_kernel, dests, across),
        in_specs=[SMEM] * 4 + [VMEM] * 3,
        out_specs=VMEM,
        out_shape=pltpu.VMEM(tile.shape, F32),
        input_output_aliases={6: 0},
        compiler_params=pltpu.CompilerParams(vmem_limit_bytes=4 * MIB),
        name="observe",
    )(row, column, counts, places, *seen, in_vmem(tile))


def finish_kernel(
    levels, is_child, nest_x, nest_y, tile, mask, in_arrived, out_arrived, in_sent, out_sent,
    out, buf, group, sems,
):
    cols = mask.shape[0]
    rows = mask.shape[2]
    chunks = rows // LANE
    step = cols * chunks
    size = levels * step
    fields = out.shape[0] // size
    blocks = cols // 3
    inner = blocks - 2
    lanes = lane_ids((levels, LANE))
    ends = jnp.logical_or(lanes == 0, lanes == LANE - 1)
    height = out_arrived.shape[0]

    def copy(f):
        at = pl.ds(f * size, size)
        return pltpu.make_async_copy(buf.at[at], out.at[at], sems.at[f])

    def piece_of(f, piece):
        return tile[pl.ds(pl.multiple_of((f * step + piece) * PAD, 8), levels), :]

    def payload(f, b, inner_ref, outer_ref):
        if b in (0, blocks - 1):
            value = outer_ref[pl.ds(f * (2 * levels) + min(b, 1), levels, stride=2), :]
        else:
            value = inner_ref[pl.ds(f * (levels * inner) + b - 1, levels, stride=inner), :]
        fixes = outer_ref[height - PAD : height - PAD + levels, :]
        shift = lax.rem(LANE - 2 * (f * cols + 3 * b), LANE)
        fixes = pltpu.roll(fixes, lax.rem(LANE + shift, LANE), 1)
        return value + jnp.where(ends, fixes, 0.0)

    def fill_child(f, carry):
        for b in range(blocks):
            high, low = halves(payload(f, b, in_arrived, out_arrived))
            both = jnp.concatenate([high, low], axis=1)
            value = jnp.dot(both, group[...], preferred_element_type=F32) * (1.0 / 9.0)
            for x in range(3 * b, 3 * b + 3):
                row = row_of(mask, x)
                for c in range(chunks):
                    piece = x * chunks + c
                    at = pl.ds(f * size + piece, levels, stride=step)
                    total = piece_of(f, piece) + value[:, chunk(c)]
                    buf[at, :] = total * row[:, chunk(c)]
        copy(f).start()
        return carry

    def fill_plain(f, carry):
        for x in range(cols):
            row = row_of(mask, x)
            for c in range(chunks):
                piece = x * chunks + c
                at = pl.ds(f * size + piece, levels, stride=step)
                buf[at, :] = piece_of(f, piece) * row[:, chunk(c)]
        return carry

    def fill_parent(f, carry):
        fill_plain(f, carry)
        for b in range(blocks):
            delta = payload(f, b, in_arrived, out_arrived) - payload(f, b, in_sent, out_sent)
            wide = jnp.concatenate([delta, jnp.zeros((levels, rows - LANE), F32)], 1)
            x = nest_x[0] + b
            value = pltpu.roll(wide, nest_y[0], 1) * row_of(mask, x)
            for c in range(chunks):
                at = pl.ds(f * size + x * chunks + c, levels, stride=step)
                buf[at, :] = buf[at, :] + value[:, chunk(c)]
        copy(f).start()
        return carry

    @pl.when(is_child[0] == 1)
    def _():
        ids = lax.broadcasted_iota(jnp.int32, group.shape, 0)
        ids = jnp.where(ids < LANE, ids, ids - LANE)
        group[...] = jnp.where(lane_ids(group.shape) // 3 == ids, 1.0, 0.0).astype(jnp.bfloat16)
        lax.fori_loop(0, fields, fill_child, 0)

    @pl.when(is_child[0] == 0)
    def _():
        lax.fori_loop(0, fields, fill_parent, 0)

    for f in range(fields):
        copy(f).wait()


def finish(is_child, nests, tile, mask, arrived, sent, dims):
    fields, levels, cols, chunks = dims
    rows = chunks * LANE
    size = (fields * levels * cols * chunks, LANE)
    return pl.pallas_call(
        functools.partial(finish_kernel, levels),
        in_specs=[SMEM] * 3 + [VMEM] * 6,
        out_specs=HBM,
        out_shape=pltpu.HBM(size, F32),
        scratch_shapes=[
            pltpu.VMEM(size, F32),
            pltpu.VMEM((2 * LANE, rows), jnp.bfloat16),
            pltpu.SemaphoreType.DMA((fields,)),
        ],
        compiler_params=pltpu.CompilerParams(vmem_limit_bytes=16 * MIB),
        cost_estimate=COST,
        name="finish",
    )(is_child, *nests, in_vmem(tile), mask, *arrived, *sent)


def from_neighbours(first, second, axis):
    size = lax.axis_size(axis)
    inner = [(i, i + 1) for i in range(1, size - 1, 2)]
    one = swapped(first, axis, 1)
    return one, lax.ppermute(second, axis, inner + [(j, i) for i, j in inner])


def swapped(value, axis, mask):
    return lax.ppermute(value, axis, [(i, i ^ mask) for i in range(lax.axis_size(axis))])


def local(
    adjoint_state,
    land_mask,
    diffusivity,
    mixing,
    nudging,
    nest_x,
    nest_y,
    obs_forcing,
    obs_cell,
    obs_count,
):
    _, fields, levels, cols, rows = adjoint_state.shape
    chunks = rows // LANE
    dims = (fields, levels, cols, chunks)
    state5 = adjoint_state.reshape(fields, levels, cols, 1, rows)
    state2 = adjoint_state.reshape(fields * levels * cols * chunks, LANE)
    mask = land_mask.reshape(cols, 1, rows)
    kappa = diffusivity.reshape(cols, 1, rows)
    mixing = mixing.reshape(fields, levels, 1, levels)
    peers, across = lax.axis_size("ty"), lax.axis_size("tx")
    assert peers == 4 and across & (across - 1) == 0 and 2 * fields * cols <= LANE
    assert levels <= PAD and cols % 3 == 0 and rows == 3 * LANE
    row = lax.axis_index("ty").astype(jnp.int32)
    column = lax.axis_index("tx").astype(jnp.int32)
    ty = row.reshape(1)
    is_child = (lax.axis_index("grp") == 0).astype(jnp.int32).reshape(1)
    nests = (nest_x, nest_y)

    forcing = obs_forcing[0, 0]
    dests = forcing.shape[1]
    counts = obs_count.reshape(1, -1)
    line = [forcing, *(swapped(forcing, "tx", n) for n in range(1, min(across, 4)))]
    for n in range(2, across.bit_length() - 1):
        blocks = jnp.concatenate(line)
        line = [blocks, swapped(blocks, "tx", 1 << n)]
    tx = column.reshape(1)
    *x_sent, ahead = x_edges(tx, state5, mask)
    ahead = ahead.reshape(-1, LANE)
    x_halos = from_neighbours(*x_sent, "tx")
    masked, matrices, parcel, in_sent, places = front(
        is_child, state2, mask, kappa, nudging, mixing, nests, line, ahead,
        obs_cell[0, :, :, 0], dims,
    )
    first = swapped(parcel, "ty", 1)
    in_arrived = swapped(in_sent, "grp", 1)
    parcel = repack(parcel, first, across * dests, PAD)
    second = swapped(parcel, "ty", 3)
    firsts = (first, second)
    masked, x_halos, parcel = lax.optimization_barrier((masked, x_halos, parcel))
    base = base_of(is_child, nests, masked, matrices, kappa, nudging, dims)
    out_sent, ahead = outer(
        is_child, tx, ty, state2, matrices, base, kappa, nudging, x_halos, firsts, nests, dims, peers
    )
    out_arrived = swapped(out_sent, "grp", 1)
    tile = tile_of(tx, ty, state2, mask, matrices, kappa, x_halos, firsts, ahead, dims, peers)
    tile = observe(ty, tx, places, counts, (parcel, second), tile, dests, across)
    arrived, sent = (in_arrived, out_arrived), (in_sent, out_sent)
    out = finish(is_child, nests, tile, mask, arrived, sent, dims)
    return out.reshape(adjoint_state.shape)


def solution(mesh):
    in_specs = (
        P("grp", None, None, "tx", "ty"),
        P("grp", "tx", "ty"),
        P("grp", "tx", "ty"),
        P("grp", None, None, None),
        P("tx", "ty"),
        P(("ty", "tx")),
        P(("ty", "tx")),
        P("grp", ("ty", "tx"), None, None),
        P("grp", None, None, ("ty", "tx")),
        P("grp", None, ("ty", "tx")),
    )
    out_specs = P("grp", None, None, "tx", "ty")
    return jax.shard_map(local, mesh=mesh, in_specs=in_specs, out_specs=out_specs, check_vma=False)
```

profile of v0, /device:TPU:9, one launch (start us, length us, event | category | flops | bytes accessed | tf_op | source)
XLA Modules:
  0.0 36.9 jit_solution(6412458303618719833)
XLA Ops:
  0.0 0.0 collective-permute-start
  0.0 2.5 %collective-permute-start.1 = (f32[16,16]{1,0:T(8,128)}, f32[16,16]{1,0:T(8,128)S(1)}, u32[]{:S(2)}, u32[]{:S(2)}) collective-permute-start(f32[16,16]{1,0:T(8,128)} %bitcast.24), channel_id=1, source_target_pairs={{0,2},{1,3},{2,0},{3,1},{4,6},{5,7},{6,4},{7,5},{8,10},{9,11},{10,... | collective-permute-start | bytes 3080 | tf_op jit(solution)/shard_map/ppermute | solution.py:817
  2.5 0.2 collective-permute-start.2
  2.7 1.7 %x_edges.1 = (f32[5,50,1,384]{3,2,1,0:T(1,128)S(1)}, f32[5,50,1,384]{3,2,1,0:T(1,128)S(1)}, f32[50,12,1,384]{3,2,1,0:T(1,128)S(1)}) custom-call(s32[1]{0:T(128)} %bitcast.2.tx.column, f32[5,50,12,1,384]{4,3,2,1,0:T(1,128)} %bitcast.28, s32[12,1,384]{2,1,0:T(1,128)} %bitcast.18), custom_call_target="tpu_custom_call" | custom-call | flops 10000000000 | bytes 100000000 | tf_op jit(solution)/shard_map/x_edges/pallas_call | solution.py:65
  4.4 1.2 %collective-permute-start.3 = (f32[5,50,1,384]{3,2,1,0:T(1,128)S(1)}, f32[5,50,1,384]{3,2,1,0:T(1,128)S(1)}, u32[]{:S(2)}, u32[]{:S(2)}) collective-permute-start(f32[5,50,1,384]{3,2,1,0:T(1,128)S(1)} %get-tuple-element.22), channel_id=1, source_target_pairs={{0,1},{1,0},{2,3},{3,2},{4,5},{5,4},{6,7},{7,6},{8,9},{9,8},{10,11... | collective-permute-start | bytes 1152008 | tf_op jit(solution)/shard_map/ppermute | solution.py:817
  5.6 4.3 %collective-permute-start.4 = (f32[5,50,1,384]{3,2,1,0:T(1,128)S(1)}, f32[5,50,1,384]{3,2,1,0:T(1,128)S(1)}, u32[]{:S(2)}, u32[]{:S(2)}) collective-permute-start(f32[5,50,1,384]{3,2,1,0:T(1,128)S(1)} %get-tuple-element.23), channel_id=1, source_target_pairs={{1,2},{2,1},{5,6},{6,5},{9,10},{10,9},{13,14},{14,13},{17,18},{18,... | collective-permute-start | bytes 1152008 | tf_op jit(solution)/shard_map/ppermute | solution.py:813
  11.1 0.0 collective-permute-done.refs_1_
  11.1 0.0 collective-permute-done.2.refs_3_
  11.2 0.0 copy-start
  11.2 0.0 copy-start.1
  11.2 4.9 %front.1 = (f32[5,12,56,384]{3,2,1,0:T(8,128)}, bf16[5,128,128]{2,1,0:T(8,128)(2,1)S(1)}, f32[72,128]{1,0:T(8,128)S(1)}, f32[500,128]{1,0:T(8,128)S(1)}, s32[16,16]{1,0:T(8,128)S(1)}) custom-call(s32[1]{0:T(128)} %bitcast.is_child, f32[9000,128]{1,0:T(8,128)} %bitcast.29, s32[12,1,384]{2,1,0:T(1,128)} %bitcast.19, f32[12,1,384]{2,1,0:T(1,128)} %bitcast.13, ...), custom_call_target="tpu_custom_call" | custom-call | flops 10000000000 | bytes 100000000 | tf_op jit(solution)/shard_map/front/pallas_call | solution.py:363
  16.1 2.1 %collective-permute-start.5 = (f32[72,128]{1,0:T(8,128)S(1)}, f32[72,128]{1,0:T(8,128)S(1)}, u32[]{:S(2)}, u32[]{:S(2)}) collective-permute-start(f32[72,128]{1,0:T(8,128)S(1)} %get-tuple-element.24.parcel), channel_id=1, source_target_pairs={{0,4},{4,0},{8,12},{12,8},{1,5},{5,1},{9,13},{13,9},{2,6},{6,2},{1... | collective-permute-start | bytes 110600 | tf_op jit(solution)/shard_map/ppermute | solution.py:817
  18.2 1.4 %collective-permute-start.7 = (f32[500,128]{1,0:T(8,128)S(1)}, f32[500,128]{1,0:T(8,128)S(1)}, u32[]{:S(2)}, u32[]{:S(2)}) collective-permute-start(f32[500,128]{1,0:T(8,128)S(1)} %get-tuple-element.31.in_sent), channel_id=1, source_target_pairs={{0,16},{16,0},{1,17},{17,1},{2,18},{18,2},{3,19},{19,3},{4,20},{20... | collective-permute-start | bytes 768008 | tf_op jit(solution)/shard_map/ppermute | solution.py:817
  19.6 0.0 collective-permute-done.5.arrived.first
  19.6 0.1 repack.1.mine
  19.7 1.5 %collective-permute-start.6 = (f32[72,128]{1,0:T(8,128)S(1)}, f32[72,128]{1,0:T(8,128)S(1)}, u32[]{:S(2)}, u32[]{:S(2)}) collective-permute-start(f32[72,128]{1,0:T(8,128)S(1)} %repack.1.mine), channel_id=1, source_target_pairs={{0,12},{4,8},{8,4},{12,0},{1,13},{5,9},{9,5},{13,1},{2,14},{6,10},... | collective-permute-start | bytes 110600 | tf_op jit(solution)/shard_map/ppermute | solution.py:817
  21.2 0.0 collective-permute-done.4.x_second
  21.2 2.9 %base.1 = f32[5,56,256]{2,1,0:T(8,128)S(1)} custom-call(s32[1]{0:T(128)} %bitcast.is_child, s32[1]{0:T(128)S(6)} %copy.15.nest_x, s32[1]{0:T(128)S(6)} %copy.16.nest_y, f32[5,12,56,384]{3,2,1,0:T(8,128)} %get-tuple-element.29.masked_in, bf16[5,128,128]{2,1,0:T(8,128)(2,1)S(1)} %get-tuple-element.26.matrices, f32[12,1,384]{2,1,0:T(1,128)S(1)} %bitcast.14, ...), custom_call_target="tpu_custom_call" | custom-call | flops 10000000000 | bytes 100000000 | tf_op jit(solution)/shard_map/base/pallas_call | solution.py:446
  24.1 0.0 copy-start.3
  24.1 1.2 %outer.1 = (f32[560,128]{1,0:T(8,128)S(1)}, f32[1800,128]{1,0:T(8,128)S(1)}) custom-call(s32[1]{0:T(128)} %bitcast.is_child, s32[1]{0:T(128)} %bitcast.2.tx.column, s32[1]{0:T(128)} %bitcast.1.ty.row, f32[9000,128]{1,0:T(8,128)} %bitcast.30, bf16[5,128,128]{2,1,0:T(8,128)(2,1)S(1)} %get-tuple-element.26.matrices, f32[5,56,256]{2,1,0:T(8,128)S(1)} %base.1, ...), custom_call_target="tpu_custom_call" | custom-call | tf_op jit(solution)/shard_map/outer/pallas_call | solution.py:575
  25.3 0.9 %collective-permute-start.8 = (f32[560,128]{1,0:T(8,128)S(1)}, f32[560,128]{1,0:T(8,128)S(1)}, u32[]{:S(2)}, u32[]{:S(2)}) collective-permute-start(f32[560,128]{1,0:T(8,128)S(1)} %get-tuple-element.32.out_sent), channel_id=1, source_target_pairs={{0,16},{16,0},{1,17},{17,1},{2,18},{18,2},{3,19},{19,3},{4,20},{20... | collective-permute-start | bytes 860168 | tf_op jit(solution)/shard_map/ppermute | solution.py:817
  26.3 5.4 %tile.1._ = f32[10080,128]{1,0:T(8,128)S(1)} custom-call(s32[1]{0:T(128)} %bitcast.2.tx.column, s32[1]{0:T(128)} %bitcast.1.ty.row, f32[9000,128]{1,0:T(8,128)} %bitcast.31, s32[12,1,384]{2,1,0:T(1,128)S(1)} %bitcast.20, bf16[5,128,128]{2,1,0:T(8,128)(2,1)S(1)} %get-tuple-element.26.matrices, f32[12,1,384]{2,1,0:T(1,128)S(1)} %bitcast.16, ...), custom_call_target="tpu_custom_call" | custom-call | flops 10000000000 | bytes 100000000 | tf_op jit(solution)/shard_map/tile/pallas_call | solution.py:643
  31.7 2.5 %observe.1.tile = f32[10080,128]{1,0:T(8,128)S(1)} custom-call(s32[1]{0:T(128)} %bitcast.1.ty.row, s32[1]{0:T(128)} %bitcast.2.tx.column, s32[1,16]{1,0:T(1,128)S(1)} %bitcast.17, s32[16,16]{1,0:T(8,128)S(1)} %get-tuple-element.20.places, f32[72,128]{1,0:T(8,128)S(1)} %repack.1.mine, ...), custom_call_target="tpu_custom_call", output_to_operand_aliasing={{}: (6, {})} | custom-call | tf_op jit(solution)/shard_map/observe/pallas_call | solution.py:693
  34.3 2.6 %finish.1 = f32[9000,128]{1,0:T(8,128)} custom-call(s32[1]{0:T(128)} %bitcast.is_child, s32[1]{0:T(128)S(6)} %copy.15.nest_x, s32[1]{0:T(128)S(6)} %copy.16.nest_y, f32[10080,128]{1,0:T(8,128)S(1)} %observe.1.tile, s32[12,1,384]{2,1,0:T(1,128)S(1)} %bitcast.21, f32[500,128]{1,0:T(8,128)S(1)} %collective-permute-done.7.in_arrived, ...), custom_call_target="tpu_custom_call" | custom-call | flops 10000000000 | bytes 100000000 | tf_op jit(solution)/shard_map/finish/pallas_call | solution.py:793
  (14 shorter events, 0.0 us)
Async XLA Ops:
  0.0 11.1 %collective-permute-start = (f32[16,16]{1,0:T(8,128)}, f32[16,16]{1,0:T(8,128)S(1)}, u32[]{:S(2)}, u32[]{:S(2)}) collective-permute-start(f32[16,16]{1,0:T(8,128)} %bitcast.23), channel_id=1, source_target_pairs={{0,1},{1,0},{2,3},{3,2},{4,5},{5,4},{6,7},{7,6},{8,9},{9,8},{10,11... | collective-permute-start | bytes 3080 | tf_op jit(solution)/shard_map/ppermute | solution.py:817
  0.0 11.1 %collective-permute-start.1 = (f32[16,16]{1,0:T(8,128)}, f32[16,16]{1,0:T(8,128)S(1)}, u32[]{:S(2)}, u32[]{:S(2)}) collective-permute-start(f32[16,16]{1,0:T(8,128)} %bitcast.24), channel_id=1, source_target_pairs={{0,2},{1,3},{2,0},{3,1},{4,6},{5,7},{6,4},{7,5},{8,10},{9,11},{10,... | collective-permute-start | bytes 3080 | tf_op jit(solution)/shard_map/ppermute | solution.py:817
  2.5 8.7 %collective-permute-start.2 = (f32[16,16]{1,0:T(8,128)}, f32[16,16]{1,0:T(8,128)S(1)}, u32[]{:S(2)}, u32[]{:S(2)}) collective-permute-start(f32[16,16]{1,0:T(8,128)} %bitcast.25), channel_id=1, source_target_pairs={{0,3},{1,2},{2,1},{3,0},{4,7},{5,6},{6,5},{7,4},{8,11},{9,10},{10,... | collective-permute-start | bytes 3080 | tf_op jit(solution)/shard_map/ppermute | solution.py:817
  2.7 8.5 %copy-start.4 = (s32[1,16,16,1]{2,3,1,0:T(1,128)S(1)}, s32[1,16,16,1]{2,3,1,0:T(1,128)}, u32[]{:S(2)}) copy-start(s32[1,16,16,1]{2,3,1,0:T(1,128)} %param.18) | copy-start | bytes 3076
  2.7 8.5 %copy-start.5 = (f32[1,1,16,16]{3,2,1,0:T(8,128)S(1)}, f32[1,1,16,16]{3,2,1,0:T(8,128)}, u32[]{:S(2)}) copy-start(f32[1,1,16,16]{3,2,1,0:T(8,128)} %param.17) | copy-start | bytes 3076
  4.4 16.8 %collective-permute-start.3 = (f32[5,50,1,384]{3,2,1,0:T(1,128)S(1)}, f32[5,50,1,384]{3,2,1,0:T(1,128)S(1)}, u32[]{:S(2)}, u32[]{:S(2)}) collective-permute-start(f32[5,50,1,384]{3,2,1,0:T(1,128)S(1)} %get-tuple-element.22), channel_id=1, source_target_pairs={{0,1},{1,0},{2,3},{3,2},{4,5},{5,4},{6,7},{7,6},{8,9},{9,8},{10,11... | collective-permute-start | bytes 1152008 | tf_op jit(solution)/shard_map/ppermute | solution.py:817
  5.6 15.6 %collective-permute-start.4 = (f32[5,50,1,384]{3,2,1,0:T(1,128)S(1)}, f32[5,50,1,384]{3,2,1,0:T(1,128)S(1)}, u32[]{:S(2)}, u32[]{:S(2)}) collective-permute-start(f32[5,50,1,384]{3,2,1,0:T(1,128)S(1)} %get-tuple-element.23), channel_id=1, source_target_pairs={{1,2},{2,1},{5,6},{6,5},{9,10},{10,9},{13,14},{14,13},{17,18},{18,... | collective-permute-start | bytes 1152008 | tf_op jit(solution)/shard_map/ppermute | solution.py:813
  11.2 10.0 %copy-start = (f32[12,384]{1,0:T(8,128)S(1)}, f32[12,384]{1,0:T(8,128)}, u32[]{:S(2)}) copy-start(f32[12,384]{1,0:T(8,128)} %nudging.5) | copy-start | bytes 55300
  11.2 10.0 %copy-start.1 = (f32[1,12,384]{2,0,1:T(1,128)S(1)}, f32[1,12,384]{2,0,1:T(1,128)}, u32[]{:S(2)}) copy-start(f32[1,12,384]{2,0,1:T(1,128)} %param.12) | copy-start | bytes 55300
  16.1 3.5 %collective-permute-start.5 = (f32[72,128]{1,0:T(8,128)S(1)}, f32[72,128]{1,0:T(8,128)S(1)}, u32[]{:S(2)}, u32[]{:S(2)}) collective-permute-start(f32[72,128]{1,0:T(8,128)S(1)} %get-tuple-element.24.parcel), channel_id=1, source_target_pairs={{0,4},{4,0},{8,12},{12,8},{1,5},{5,1},{9,13},{13,9},{2,6},{6,2},{1... | collective-permute-start | bytes 110600 | tf_op jit(solution)/shard_map/ppermute | solution.py:817
  18.2 16.0 %collective-permute-start.7 = (f32[500,128]{1,0:T(8,128)S(1)}, f32[500,128]{1,0:T(8,128)S(1)}, u32[]{:S(2)}, u32[]{:S(2)}) collective-permute-start(f32[500,128]{1,0:T(8,128)S(1)} %get-tuple-element.31.in_sent), channel_id=1, source_target_pairs={{0,16},{16,0},{1,17},{17,1},{2,18},{18,2},{3,19},{19,3},{4,20},{20... | collective-permute-start | bytes 768008 | tf_op jit(solution)/shard_map/ppermute | solution.py:817
  19.7 4.4 %collective-permute-start.6 = (f32[72,128]{1,0:T(8,128)S(1)}, f32[72,128]{1,0:T(8,128)S(1)}, u32[]{:S(2)}, u32[]{:S(2)}) collective-permute-start(f32[72,128]{1,0:T(8,128)S(1)} %repack.1.mine), channel_id=1, source_target_pairs={{0,12},{4,8},{8,4},{12,0},{1,13},{5,9},{9,5},{13,1},{2,14},{6,10},... | collective-permute-start | bytes 110600 | tf_op jit(solution)/shard_map/ppermute | solution.py:817
  24.1 2.2 %copy-start.3 = (s32[1,12,384]{2,0,1:T(1,128)S(1)}, s32[1,12,384]{2,0,1:T(1,128)}, u32[]{:S(2)}) copy-start(s32[1,12,384]{2,0,1:T(1,128)} %param.11) | copy-start | bytes 55300
  25.3 8.9 %collective-permute-start.8 = (f32[560,128]{1,0:T(8,128)S(1)}, f32[560,128]{1,0:T(8,128)S(1)}, u32[]{:S(2)}, u32[]{:S(2)}) collective-permute-start(f32[560,128]{1,0:T(8,128)S(1)} %get-tuple-element.32.out_sent), channel_id=1, source_target_pairs={{0,16},{16,0},{1,17},{17,1},{2,18},{18,2},{3,19},{19,3},{4,20},{20... | collective-permute-start | bytes 860168 | tf_op jit(solution)/shard_map/ppermute | solution.py:817
  26.3 5.5 %copy-start.2 = (s32[1,16,1]{1,2,0:T(1,128)S(1)}, s32[1,16,1]{1,2,0:T(1,128)}, u32[]{:S(2)}) copy-start(s32[1,16,1]{1,2,0:T(1,128)} %param.19) | copy-start | bytes 196
where the time goes:
time: 37.1 us; the launch traced here: 36.9 us
  Pallas kernels  21.3 us (57%)
  starting transfers between devices  14 us (38%)
  between operations  1.47 us (4%)
    ppermute x8, starting transfers between devices, swapped(): lax.ppermute(value, axis, [(i, i ^ mask) for i in range(lax.axis_size(axi...  9.77 us
    pallas_call x1, Pallas kernels, tile_of(): pl.pallas_call(functools.partial(tile_kernel, levels, peers), in_specs=[S...  5.44 us
    pallas_call x1, Pallas kernels, front(): pl.pallas_call(functools.partial(front_kernel, levels, bs, slots), in_spe...  4.9 us
    ppermute x1, starting transfers between devices, from_neighbours(): return (one, lax.ppermute(second, axis, inner + [(j, i) for i, j in inner]))  4.26 us
    pallas_call x1, Pallas kernels, base_of(): pl.pallas_call(functools.partial(base_kernel, levels, bs), in_specs=[SMEM...  2.88 us
    pallas_call x1, Pallas kernels, finish(): pl.pallas_call(functools.partial(finish_kernel, levels), in_specs=[SMEM]...  2.61 us
    pallas_call x1, Pallas kernels, observe(): pl.pallas_call(functools.partial(observe_kernel, dests, across), in_specs...  2.52 us
    pallas_call x1, Pallas kernels, x_edges(): pl.pallas_call(x_edges_kernel, in_specs=[SMEM, HBM, HBM], out_specs=[VMEM...  1.69 us
  transfers between devices with their start and end apart: 9, of which 0 were waited for; matrix products, arithmetic and copies ran while one was open for 0% of the time, Pallas kernels for 51%

commit v1 on v0

--- a/solution.py
+++ b/solution.py
@@ -191,13 +191,13 @@
             weights[at + 3 : at + 4, :] = value
 
 
-def child_rows(f, bs, masked, weights, wide):
+def child_rows(f, g, bs, masked, weights, wide):
     cols, _, rows = masked.shape[1:]
     for i, b in enumerate(bs):
 
         def term(n, x):
             at = i * TERMS + n
-            return weights[at : at + 1, :] * masked[f, x]
+            return weights[at : at + 1, :] * masked[g, x]
 
         total = None
         for n, x in enumerate(range(3 * b - 1, 3 * b + 4)):
@@ -210,18 +210,18 @@
         wide[at, :rows], wide[at, rows:] = halves(deepened(total))
 
 
-def parent_rows(f, bs, nest_x, nest_y, masked, kappa, stack):
+def parent_rows(f, g, bs, nest_x, nest_y, masked, kappa, stack):
     cols, _, rows = masked.shape[1:]
     back = lax.rem(rows - nest_y[0], rows)
     for i, b in enumerate(bs):
         x = nest_x[0] + b
-        above = masked[f, jnp.maximum(x - 1, 0)]
-        below = masked[f, jnp.minimum(x + 1, cols - 1)]
+        above = masked[g, jnp.maximum(x - 1, 0)]
+        below = masked[g, jnp.minimum(x + 1, cols - 1)]
         if b == 0:
             above = jnp.where(x == 0, 0.0, above)
         if b == cols // 3 - 1:
             below = jnp.where(x == cols - 1, 0.0, below)
-        value = spread_of(masked[f, x], above, below, kappa[x])
+        value = spread_of(masked[g, x], above, below, kappa[x])
         value = deepened(pltpu.roll(value, back, 1)[:, :LANE])
         fill_stack(stack.at[f], chunk(i), value)
 
@@ -250,7 +250,7 @@
     ]
 
 
-ROOM = 18
+ROOM = 19
 
 
 def front_kernel(
@@ -266,7 +266,7 @@
 
 def front_steps(
     levels, bs, slots, line, is_child, state, mask, kappa, nudging, mixing, nest_x, nest_y, ahead,
-    cells, masked_out, matrices, parcel, inner, places,
+    cells, masked_out, lead, matrices, parcel, inner, places,
     buf, masked, mask_buf, kappa_buf, nudging_buf, mixing_buf, square, weights, wide, stack, group, sems, out_sems,
 ):
     fields, cols, _, rows = masked.shape
@@ -311,23 +311,24 @@
 
     def field(f, total_edges, first=False):
         fill_matrix(levels, mixing_buf[f, :, 0, :], square, matrices.at[f])
+        here, g = (lead, 0) if first else (masked, f)
         if first:
-            fill_masked(levels, ahead, f, mask_buf, masked.at[f])
+            fill_masked(levels, ahead, f, mask_buf, lead.at[0])
         else:
             copy(f).wait()
             fill_masked(levels, buf, f, mask_buf, masked.at[f])
-        copy_out(f).start()
+            copy_out(f).start()
         own_edges = packed(
-            lambda x: (masked[f, x, :, :LANE], masked[f, x, :, rows - LANE :]), cols
+            lambda x: (here[g, x, :, :LANE], here[g, x, :, rows - LANE :]), cols
         )
 
         @pl.when(is_child[0] == 1)
         def _():
-            child_rows(f, bs, masked, weights, wide)
+            child_rows(f, g, bs, here, weights, wide)
 
         @pl.when(is_child[0] == 0)
         def _():
-            parent_rows(f, bs, nest_x, nest_y, masked, kappa_buf, stack)
+            parent_rows(f, g, bs, nest_x, nest_y, here, kappa_buf, stack)
 
         return total_edges + pltpu.roll(own_edges, 2 * f * cols, 1)
 
@@ -349,7 +350,7 @@
             inner[at, :] = mixed[:levels, chunk(i)]
 
     mix_rows(bs, is_child, wide, group, stack, matrices, emit)
-    for f in range(fields):
+    for f in range(1, fields):
         copy_out(f).wait()
 
 
@@ -363,9 +364,10 @@
     return pl.pallas_call(
         functools.partial(front_kernel, levels, bs, slots),
         in_specs=[SMEM] + [HBM] * 5 + [SMEM] * 2 + [VMEM] * (2 + len(line)),
-        out_specs=[HBM] + [VMEM] * 4,
+        out_specs=[HBM] + [VMEM] * 5,
         out_shape=[
             pltpu.HBM((fields, cols, PAD, rows), F32),
+            pltpu.VMEM((1, cols, PAD, rows), F32),
             pltpu.VMEM((fields, 2 * DEPTH, 2 * DEPTH), jnp.bfloat16),
             pltpu.VMEM((PAD + height, LANE), F32),
             pltpu.VMEM((fields * levels * len(bs), LANE), F32),
@@ -389,7 +391,7 @@
 
 
 def base_kernel(
-    levels, bs, is_child, nest_x, nest_y, masked_in, matrices, kappa, nudging, base,
+    levels, bs, is_child, nest_x, nest_y, masked_in, lead, matrices, kappa, nudging, base,
     masked, weights, wide, stack, group, sems,
 ):
     fields, cols = masked.shape[:2]
@@ -407,7 +409,7 @@
 
     @pl.when(is_child[0] == 1)
     def _():
-        for f in range(fields):
+        for f in range(1, fields):
             for copy in child_copies(f):
                 copy.start()
         fill_group(group)
@@ -416,22 +418,24 @@
         def field(f, carry):
             for copy in child_copies(f):
                 copy.wait()
-            child_rows(f, bs, masked, weights, wide)
+            child_rows(f, f, bs, masked, weights, wide)
             return carry
 
-        lax.fori_loop(0, fields, field, 0)
+        child_rows(0, 0, bs, lead, weights, wide)
+        lax.fori_loop(1, fields, field, 0)
 
     @pl.when(is_child[0] == 0)
     def _():
-        for f in range(fields):
+        for f in range(1, fields):
             parent_copy(f).start()
 
         def field(f, carry):
             parent_copy(f).wait()
-            parent_rows(f, bs, nest_x, nest_y, masked, kappa, stack)
+            parent_rows(f, f, bs, nest_x, nest_y, masked, kappa, stack)
             return carry
 
-        lax.fori_loop(0, fields, field, 0)
+        parent_rows(0, 0, bs, nest_x, nest_y, lead, kappa, stack)
+        lax.fori_loop(1, fields, field, 0)
 
     def emit(f, mixed):
         base[f, :, :] = mixed[:PAD, :]
@@ -439,13 +443,13 @@
     mix_rows(bs, is_child, wide, group, stack, matrices, emit)
 
 
-def base_of(is_child, nests, masked, matrices, kappa, nudging, dims):
+def base_of(is_child, nests, masked, lead, matrices, kappa, nudging, dims):
     fields, levels, cols, chunks = dims
     rows = chunks * LANE
     bs = (0, cols // 3 - 1)
     return pl.pallas_call(
         functools.partial(base_kernel, levels, bs),
-        in_specs=[SMEM] * 3 + [HBM] + [VMEM] * 3,
+        in_specs=[SMEM] * 3 + [HBM] + [VMEM] * 4,
         out_specs=VMEM,
         out_shape=pltpu.VMEM((fields, PAD, 2 * LANE), F32),
         scratch_shapes=[pltpu.VMEM(masked.shape, F32)]
@@ -454,7 +458,7 @@
         compiler_params=pltpu.CompilerParams(vmem_limit_bytes=16 * MIB),
         cost_estimate=COST,
         name="base",
-    )(is_child, *nests, in_hbm(masked), matrices, kappa, nudging)
+    )(is_child, *nests, in_hbm(masked), in_vmem(lead), matrices, kappa, nudging)
 
 
 def merged(own, other, width):
@@ -671,22 +675,27 @@
         lane_in = lax.rem(g, LANE // dests) * dests + me
         block = PAD + lax.div(g, LANE // dests) * slots
         count = counts[0, origin]
-        for k in range(0, slots, 2):
+        for k0 in range(0, slots, 4):
             ats, adds = [], []
-            for m in range(k, k + 2):
+            for m in range(k0, k0 + 4):
                 place = places[origin, m]
                 lane = place & (LANE - 1)
                 value = pltpu.roll(ref[pl.ds(block + m, 1), :], (lane - lane_in) & (LANE - 1), 1)
                 ats.append(place >> 7)
                 adds.append(jnp.where(lanes == jnp.where(m < count, lane, LANE), value, 0.0))
             olds = [tile[pl.ds(at, 1), :] for at in ats]
-            also = jnp.where(ats[0] == ats[1], adds[0], 0.0)
-            tile[pl.ds(ats[0], 1), :] = olds[0] + adds[0]
-            tile[pl.ds(ats[1], 1), :] = olds[1] + adds[1] + also
+            for k, (at, total) in enumerate(zip(ats, olds)):
+                total = total + adds[k]
+                for j in range(k):
+                    total = total + jnp.where(ats[j] == at, adds[j], 0.0)
+                tile[pl.ds(at, 1), :] = total
         return carry
 
-    lax.fori_loop(0, half, functools.partial(source, 0, mine), 0)
-    lax.fori_loop(0, half, functools.partial(source, 3, theirs), 0)
+    def both(n, carry):
+        source(0, mine, n, carry)
+        return source(3, theirs, n, carry)
+
+    lax.fori_loop(0, half, both, 0)
 
 
 def observe(row, column, places, counts, seen, tile, dests, across):
@@ -857,7 +866,7 @@
     *x_sent, ahead = x_edges(tx, state5, mask)
     ahead = ahead.reshape(-1, LANE)
     x_halos = from_neighbours(*x_sent, "tx")
-    masked, matrices, parcel, in_sent, places = front(
+    masked, lead, matrices, parcel, in_sent, places = front(
         is_child, state2, mask, kappa, nudging, mixing, nests, line, ahead,
         obs_cell[0, :, :, 0], dims,
     )
@@ -867,7 +876,7 @@
     second = swapped(parcel, "ty", 3)
     firsts = (first, second)
     masked, x_halos, parcel = lax.optimization_barrier((masked, x_halos, parcel))
-    base = base_of(is_child, nests, masked, matrices, kappa, nudging, dims)
+    base = base_of(is_child, nests, masked, lead, matrices, kappa, nudging, dims)
     out_sent, ahead = outer(
         is_child, tx, ty, state2, matrices, base, kappa, nudging, x_halos, firsts, nests, dims, peers
     )

time: 37.1 us -> 38.8 us (1.046)
  local copies, waits for them, and re-layouts: 0.03 us -> 2.2 us
  Pallas kernels: 21.3 us -> 20.8 us
    unnamed x12 -> x16, local copies, waits for them, and re-layouts: 0.03 us -> 2.2 us
    pallas_call x1, Pallas kernels: 2.52 us -> 2.13 us  [observe(): pl.pallas_call(functools.partial(observe_kernel, dests, across), in_specs...]
  transfers between devices with their start and end apart: 9 -> 9, of which waited for: 0 -> 0; matrix products, arithmetic and copies ran while one was open for 0% -> 0% of each run, Pallas kernels for 51% -> 47%
where the time goes in v1:
time: 38.8 us; the launch traced here: 38.5 us
  Pallas kernels  20.8 us (54%)
  starting transfers between devices  14 us (36%)
  local copies, waits for them, and re-layouts  2.2 us (6%)
  between operations  1.49 us (4%)
    ppermute x8, starting transfers between devices, swapped(): lax.ppermute(value, axis, [(i, i ^ mask) for i in range(lax.axis_size(axi...  9.75 us
    pallas_call x1, Pallas kernels, tile_of(): pl.pallas_call(functools.partial(tile_kernel, levels, peers), in_specs=[S...  5.44 us
    pallas_call x1, Pallas kernels, front(): pl.pallas_call(functools.partial(front_kernel, levels, bs, slots), in_spe...  4.93 us
    ppermute x1, starting transfers between devices, from_neighbours(): return (one, lax.ppermute(second, axis, inner + [(j, i) for i, j in inner]))  4.26 us
    pallas_call x1, Pallas kernels, base_of(): pl.pallas_call(functools.partial(base_kernel, levels, bs), in_specs=[SMEM...  2.73 us
    pallas_call x1, Pallas kernels, finish(): pl.pallas_call(functools.partial(finish_kernel, levels), in_specs=[SMEM]...  2.61 us
    unnamed x16, local copies, waits for them, and re-layouts  2.2 us
    pallas_call x1, Pallas kernels, observe(): pl.pallas_call(functools.partial(observe_kernel, dests, across), in_specs...  2.13 us
  transfers between devices with their start and end apart: 9, of which 0 were waited for; matrix products, arithmetic and copies ran while one was open for 0% of the time, Pallas kernels for 47%

profile of v1, /device:TPU:9, one launch (start us, length us, event | category | flops | bytes accessed | tf_op | source)
XLA Modules:
  0.0 38.5 jit_solution(16504100707430808096)
XLA Ops:
  0.0 2.5 %collective-permute-start.1 = (f32[16,16]{1,0:T(8,128)}, f32[16,16]{1,0:T(8,128)S(1)}, u32[]{:S(2)}, u32[]{:S(2)}) collective-permute-start(f32[16,16]{1,0:T(8,128)} %bitcast.24), channel_id=1, source_target_pairs={{0,2},{1,3},{2,0},{3,1},{4,6},{5,7},{6,4},{7,5},{8,10},{9,11},{10,... | collective-permute-start | bytes 3080 | tf_op jit(solution)/shard_map/ppermute | solution.py:826
  2.5 0.2 collective-permute-start.2
  2.7 1.7 %x_edges.1 = (f32[5,50,1,384]{3,2,1,0:T(1,128)S(1)}, f32[5,50,1,384]{3,2,1,0:T(1,128)S(1)}, f32[50,12,1,384]{3,2,1,0:T(1,128)S(1)}) custom-call(s32[1]{0:T(128)} %bitcast.2.tx.column, f32[5,50,12,1,384]{4,3,2,1,0:T(1,128)} %bitcast.28, s32[12,1,384]{2,1,0:T(1,128)} %bitcast.18), custom_call_target="tpu_custom_call" | custom-call | flops 10000000000 | bytes 100000000 | tf_op jit(solution)/shard_map/x_edges/pallas_call | solution.py:65
  4.4 1.2 %collective-permute-start.3 = (f32[5,50,1,384]{3,2,1,0:T(1,128)S(1)}, f32[5,50,1,384]{3,2,1,0:T(1,128)S(1)}, u32[]{:S(2)}, u32[]{:S(2)}) collective-permute-start(f32[5,50,1,384]{3,2,1,0:T(1,128)S(1)} %get-tuple-element.23), channel_id=1, source_target_pairs={{0,1},{1,0},{2,3},{3,2},{4,5},{5,4},{6,7},{7,6},{8,9},{9,8},{10,11... | collective-permute-start | bytes 1152008 | tf_op jit(solution)/shard_map/ppermute | solution.py:826
  5.6 4.3 %collective-permute-start.4 = (f32[5,50,1,384]{3,2,1,0:T(1,128)S(1)}, f32[5,50,1,384]{3,2,1,0:T(1,128)S(1)}, u32[]{:S(2)}, u32[]{:S(2)}) collective-permute-start(f32[5,50,1,384]{3,2,1,0:T(1,128)S(1)} %get-tuple-element.24), channel_id=1, source_target_pairs={{1,2},{2,1},{5,6},{6,5},{9,10},{10,9},{13,14},{14,13},{17,18},{18,... | collective-permute-start | bytes 1152008 | tf_op jit(solution)/shard_map/ppermute | solution.py:822
  11.1 0.0 collective-permute-done.refs_1_
  11.2 0.0 copy-start
  11.2 0.0 copy-start.1
  11.2 4.9 %front.1 = (f32[5,12,56,384]{3,2,1,0:T(8,128)}, f32[1,12,56,384]{3,2,1,0:T(8,128)S(1)}, bf16[5,128,128]{2,1,0:T(8,128)(2,1)S(1)}, f32[72,128]{1,0:T(8,128)S(1)},...) custom-call(s32[1]{0:T(128)} %bitcast.is_child, f32[9000,128]{1,0:T(8,128)} %bitcast.29, s32[12,1,384]{2,1,0:T(1,128)} %bitcast.19, ...), custom_call_target="tpu_custom_call" | custom-call | flops 10000000000 | bytes 100000000 | tf_op jit(solution)/shard_map/front/pallas_call | solution.py:364
  16.1 0.0 copy-start.6
  16.1 1.0 %copy-done.6 = f32[1,12,56,384]{3,2,1,0:T(8,128)} copy-done((f32[1,12,56,384]{3,2,1,0:T(8,128)}, f32[1,12,56,384]{3,2,1,0:T(8,128)S(1)}, u32[]{:S(2)}) %copy-start.6) | copy-done | bytes 1032216
  17.1 2.1 %collective-permute-start.5 = (f32[72,128]{1,0:T(8,128)S(1)}, f32[72,128]{1,0:T(8,128)S(1)}, u32[]{:S(2)}, u32[]{:S(2)}) collective-permute-start(f32[72,128]{1,0:T(8,128)S(1)} %get-tuple-element.25.parcel), channel_id=1, source_target_pairs={{0,4},{4,0},{8,12},{12,8},{1,5},{5,1},{9,13},{13,9},{2,6},{6,2},{1... | collective-permute-start | bytes 110600 | tf_op jit(solution)/shard_map/ppermute | solution.py:826
  19.2 1.3 %collective-permute-start.7 = (f32[500,128]{1,0:T(8,128)S(1)}, f32[500,128]{1,0:T(8,128)S(1)}, u32[]{:S(2)}, u32[]{:S(2)}) collective-permute-start(f32[500,128]{1,0:T(8,128)S(1)} %get-tuple-element.33.in_sent), channel_id=1, source_target_pairs={{0,16},{16,0},{1,17},{17,1},{2,18},{18,2},{3,19},{19,3},{4,20},{20... | collective-permute-start | bytes 768008 | tf_op jit(solution)/shard_map/ppermute | solution.py:826
  20.5 0.1 repack.1.mine
  20.6 1.4 %collective-permute-start.6 = (f32[72,128]{1,0:T(8,128)S(1)}, f32[72,128]{1,0:T(8,128)S(1)}, u32[]{:S(2)}, u32[]{:S(2)}) collective-permute-start(f32[72,128]{1,0:T(8,128)S(1)} %repack.1.mine), channel_id=1, source_target_pairs={{0,12},{4,8},{8,4},{12,0},{1,13},{5,9},{9,5},{13,1},{2,14},{6,10},... | collective-permute-start | bytes 110600 | tf_op jit(solution)/shard_map/ppermute | solution.py:826
  22.0 0.0 copy-start.7
  22.0 1.2 %copy-done.7 = f32[1,12,56,384]{3,2,1,0:T(8,128)S(1)} copy-done((f32[1,12,56,384]{3,2,1,0:T(8,128)S(1)}, f32[1,12,56,384]{3,2,1,0:T(8,128)}, u32[]{:S(2)}) %copy-start.7) | copy-done | bytes 1032216
  23.3 2.7 %base.1 = f32[5,56,256]{2,1,0:T(8,128)S(1)} custom-call(s32[1]{0:T(128)} %bitcast.is_child, s32[1]{0:T(128)S(6)} %copy.15.nest_x, s32[1]{0:T(128)S(6)} %copy.16.nest_y, f32[5,12,56,384]{3,2,1,0:T(8,128)} %get-tuple-element.30.masked_in, f32[1,12,56,384]{3,2,1,0:T(8,128)S(1)} %copy-done.7, bf16[5,128,128]{2,1,0:T(8,128)(2,1)S(1)} %get-tuple-element.27.matrices, ...), custom_call_target="tpu_custom_call" | custom-call | flops 10000000000 | bytes 100000000 | tf_op jit(solution)/shard_map/base/pallas_call | solution.py:450
  26.0 0.0 copy-start.3
  26.0 1.2 %outer.1 = (f32[560,128]{1,0:T(8,128)S(1)}, f32[1800,128]{1,0:T(8,128)S(1)}) custom-call(s32[1]{0:T(128)} %bitcast.is_child, s32[1]{0:T(128)} %bitcast.2.tx.column, s32[1]{0:T(128)} %bitcast.1.ty.row, f32[9000,128]{1,0:T(8,128)} %bitcast.30, bf16[5,128,128]{2,1,0:T(8,128)(2,1)S(1)} %get-tuple-element.27.matrices, f32[5,56,256]{2,1,0:T(8,128)S(1)} %base.1, ...), custom_call_target="tpu_custom_call" | custom-call | tf_op jit(solution)/shard_map/outer/pallas_call | solution.py:579
  27.2 1.1 %collective-permute-start.8 = (f32[560,128]{1,0:T(8,128)S(1)}, f32[560,128]{1,0:T(8,128)S(1)}, u32[]{:S(2)}, u32[]{:S(2)}) collective-permute-start(f32[560,128]{1,0:T(8,128)S(1)} %get-tuple-element.34.out_sent), channel_id=1, source_target_pairs={{0,16},{16,0},{1,17},{17,1},{2,18},{18,2},{3,19},{19,3},{4,20},{20... | collective-permute-start | bytes 860168 | tf_op jit(solution)/shard_map/ppermute | solution.py:826
  28.3 5.4 %tile.1._ = f32[10080,128]{1,0:T(8,128)S(1)} custom-call(s32[1]{0:T(128)} %bitcast.2.tx.column, s32[1]{0:T(128)} %bitcast.1.ty.row, f32[9000,128]{1,0:T(8,128)} %bitcast.31, s32[12,1,384]{2,1,0:T(1,128)S(1)} %bitcast.20, bf16[5,128,128]{2,1,0:T(8,128)(2,1)S(1)} %get-tuple-element.27.matrices, f32[12,1,384]{2,1,0:T(1,128)S(1)} %bitcast.16, ...), custom_call_target="tpu_custom_call" | custom-call | flops 10000000000 | bytes 100000000 | tf_op jit(solution)/shard_map/tile/pallas_call | solution.py:647
  33.8 2.1 %observe.1.tile = f32[10080,128]{1,0:T(8,128)S(1)} custom-call(s32[1]{0:T(128)} %bitcast.1.ty.row, s32[1]{0:T(128)} %bitcast.2.tx.column, s32[1,16]{1,0:T(1,128)S(1)} %bitcast.17, s32[16,16]{1,0:T(8,128)S(1)} %get-tuple-element.21.places, f32[72,128]{1,0:T(8,128)S(1)} %repack.1.mine, ...), custom_call_target="tpu_custom_call", output_to_operand_aliasing={{}: (6, {})} | custom-call | tf_op jit(solution)/shard_map/observe/pallas_call | solution.py:702
  35.9 2.6 %finish.1 = f32[9000,128]{1,0:T(8,128)} custom-call(s32[1]{0:T(128)} %bitcast.is_child, s32[1]{0:T(128)S(6)} %copy.15.nest_x, s32[1]{0:T(128)S(6)} %copy.16.nest_y, f32[10080,128]{1,0:T(8,128)S(1)} %observe.1.tile, s32[12,1,384]{2,1,0:T(1,128)S(1)} %bitcast.21, f32[500,128]{1,0:T(8,128)S(1)} %collective-permute-done.7.in_arrived, ...), custom_call_target="tpu_custom_call" | custom-call | flops 10000000000 | bytes 100000000 | tf_op jit(solution)/shard_map/finish/pallas_call | solution.py:802
  (18 shorter events, 0.0 us)
Async XLA Ops:
  0.0 11.1 %collective-permute-start = (f32[16,16]{1,0:T(8,128)}, f32[16,16]{1,0:T(8,128)S(1)}, u32[]{:S(2)}, u32[]{:S(2)}) collective-permute-start(f32[16,16]{1,0:T(8,128)} %bitcast.23), channel_id=1, source_target_pairs={{0,1},{1,0},{2,3},{3,2},{4,5},{5,4},{6,7},{7,6},{8,9},{9,8},{10,11... | collective-permute-start | bytes 3080 | tf_op jit(solution)/shard_map/ppermute | solution.py:826
  0.0 11.1 %collective-permute-start.1 = (f32[16,16]{1,0:T(8,128)}, f32[16,16]{1,0:T(8,128)S(1)}, u32[]{:S(2)}, u32[]{:S(2)}) collective-permute-start(f32[16,16]{1,0:T(8,128)} %bitcast.24), channel_id=1, source_target_pairs={{0,2},{1,3},{2,0},{3,1},{4,6},{5,7},{6,4},{7,5},{8,10},{9,11},{10,... | collective-permute-start | bytes 3080 | tf_op jit(solution)/shard_map/ppermute | solution.py:826
  2.5 8.7 %collective-permute-start.2 = (f32[16,16]{1,0:T(8,128)}, f32[16,16]{1,0:T(8,128)S(1)}, u32[]{:S(2)}, u32[]{:S(2)}) collective-permute-start(f32[16,16]{1,0:T(8,128)} %bitcast.25), channel_id=1, source_target_pairs={{0,3},{1,2},{2,1},{3,0},{4,7},{5,6},{6,5},{7,4},{8,11},{9,10},{10,... | collective-permute-start | bytes 3080 | tf_op jit(solution)/shard_map/ppermute | solution.py:826
  2.7 8.5 %copy-start.4 = (s32[1,16,16,1]{2,3,1,0:T(1,128)S(1)}, s32[1,16,16,1]{2,3,1,0:T(1,128)}, u32[]{:S(2)}) copy-start(s32[1,16,16,1]{2,3,1,0:T(1,128)} %param.18) | copy-start | bytes 3076
  2.7 8.5 %copy-start.5 = (f32[1,1,16,16]{3,2,1,0:T(8,128)S(1)}, f32[1,1,16,16]{3,2,1,0:T(8,128)}, u32[]{:S(2)}) copy-start(f32[1,1,16,16]{3,2,1,0:T(8,128)} %param.17) | copy-start | bytes 3076
  4.4 17.7 %collective-permute-start.3 = (f32[5,50,1,384]{3,2,1,0:T(1,128)S(1)}, f32[5,50,1,384]{3,2,1,0:T(1,128)S(1)}, u32[]{:S(2)}, u32[]{:S(2)}) collective-permute-start(f32[5,50,1,384]{3,2,1,0:T(1,128)S(1)} %get-tuple-element.23), channel_id=1, source_target_pairs={{0,1},{1,0},{2,3},{3,2},{4,5},{5,4},{6,7},{7,6},{8,9},{9,8},{10,11... | collective-permute-start | bytes 1152008 | tf_op jit(solution)/shard_map/ppermute | solution.py:826
  5.6 16.5 %collective-permute-start.4 = (f32[5,50,1,384]{3,2,1,0:T(1,128)S(1)}, f32[5,50,1,384]{3,2,1,0:T(1,128)S(1)}, u32[]{:S(2)}, u32[]{:S(2)}) collective-permute-start(f32[5,50,1,384]{3,2,1,0:T(1,128)S(1)} %get-tuple-element.24), channel_id=1, source_target_pairs={{1,2},{2,1},{5,6},{6,5},{9,10},{10,9},{13,14},{14,13},{17,18},{18,... | collective-permute-start | bytes 1152008 | tf_op jit(solution)/shard_map/ppermute | solution.py:822
  11.2 10.8 %copy-start = (f32[12,384]{1,0:T(8,128)S(1)}, f32[12,384]{1,0:T(8,128)}, u32[]{:S(2)}) copy-start(f32[12,384]{1,0:T(8,128)} %nudging.5) | copy-start | bytes 55300
  11.2 10.8 %copy-start.1 = (f32[1,12,384]{2,0,1:T(1,128)S(1)}, f32[1,12,384]{2,0,1:T(1,128)}, u32[]{:S(2)}) copy-start(f32[1,12,384]{2,0,1:T(1,128)} %param.12) | copy-start | bytes 55300
  16.1 1.0 %copy-start.6 = (f32[1,12,56,384]{3,2,1,0:T(8,128)}, f32[1,12,56,384]{3,2,1,0:T(8,128)S(1)}, u32[]{:S(2)}) copy-start(f32[1,12,56,384]{3,2,1,0:T(8,128)S(1)} %get-tuple-element.31.lead) | copy-start | bytes 3096580
  17.1 3.4 %collective-permute-start.5 = (f32[72,128]{1,0:T(8,128)S(1)}, f32[72,128]{1,0:T(8,128)S(1)}, u32[]{:S(2)}, u32[]{:S(2)}) collective-permute-start(f32[72,128]{1,0:T(8,128)S(1)} %get-tuple-element.25.parcel), channel_id=1, source_target_pairs={{0,4},{4,0},{8,12},{12,8},{1,5},{5,1},{9,13},{13,9},{2,6},{6,2},{1... | collective-permute-start | bytes 110600 | tf_op jit(solution)/shard_map/ppermute | solution.py:826
  19.2 16.7 %collective-permute-start.7 = (f32[500,128]{1,0:T(8,128)S(1)}, f32[500,128]{1,0:T(8,128)S(1)}, u32[]{:S(2)}, u32[]{:S(2)}) collective-permute-start(f32[500,128]{1,0:T(8,128)S(1)} %get-tuple-element.33.in_sent), channel_id=1, source_target_pairs={{0,16},{16,0},{1,17},{17,1},{2,18},{18,2},{3,19},{19,3},{4,20},{20... | collective-permute-start | bytes 768008 | tf_op jit(solution)/shard_map/ppermute | solution.py:826
  20.6 5.4 %collective-permute-start.6 = (f32[72,128]{1,0:T(8,128)S(1)}, f32[72,128]{1,0:T(8,128)S(1)}, u32[]{:S(2)}, u32[]{:S(2)}) collective-permute-start(f32[72,128]{1,0:T(8,128)S(1)} %repack.1.mine), channel_id=1, source_target_pairs={{0,12},{4,8},{8,4},{12,0},{1,13},{5,9},{9,5},{13,1},{2,14},{6,10},... | collective-permute-start | bytes 110600 | tf_op jit(solution)/shard_map/ppermute | solution.py:826
  22.0 1.2 %copy-start.7 = (f32[1,12,56,384]{3,2,1,0:T(8,128)S(1)}, f32[1,12,56,384]{3,2,1,0:T(8,128)}, u32[]{:S(2)}) copy-start(f32[1,12,56,384]{3,2,1,0:T(8,128)} %copy-done.6) | copy-start | bytes 3096580
  26.0 2.3 %copy-start.3 = (s32[1,12,384]{2,0,1:T(1,128)S(1)}, s32[1,12,384]{2,0,1:T(1,128)}, u32[]{:S(2)}) copy-start(s32[1,12,384]{2,0,1:T(1,128)} %param.11) | copy-start | bytes 55300
  27.2 8.7 %collective-permute-start.8 = (f32[560,128]{1,0:T(8,128)S(1)}, f32[560,128]{1,0:T(8,128)S(1)}, u32[]{:S(2)}, u32[]{:S(2)}) collective-permute-start(f32[560,128]{1,0:T(8,128)S(1)} %get-tuple-element.34.out_sent), channel_id=1, source_target_pairs={{0,16},{16,0},{1,17},{17,1},{2,18},{18,2},{3,19},{19,3},{4,20},{20... | collective-permute-start | bytes 860168 | tf_op jit(solution)/shard_map/ppermute | solution.py:826
  28.3 5.4 %copy-start.2 = (s32[1,16,1]{1,2,0:T(1,128)S(1)}, s32[1,16,1]{1,2,0:T(1,128)}, u32[]{:S(2)}) copy-start(s32[1,16,1]{1,2,0:T(1,128)} %param.19) | copy-start | bytes 196

commit v2 on v0

--- a/solution.py
+++ b/solution.py
@@ -457,6 +457,22 @@
     )(is_child, *nests, in_hbm(masked), matrices, kappa, nudging)
 
 
+def stacked_kernel(one, two, out):
+    out[: one.shape[0], :] = one[...]
+    out[one.shape[0] :, :] = two[...]
+
+
+def stacked(one, two):
+    return pl.pallas_call(
+        stacked_kernel,
+        in_specs=[VMEM] * 2,
+        out_specs=VMEM,
+        out_shape=pltpu.VMEM((2 * one.shape[0], one.shape[1]), F32),
+        compiler_params=pltpu.CompilerParams(vmem_limit_bytes=4 * MIB),
+        name="stacked",
+    )(one, two)
+
+
 def merged(own, other, width):
     if 2 * width <= LANE:
         return own + pltpu.roll(other, width, 1)
@@ -671,22 +687,27 @@
         lane_in = lax.rem(g, LANE // dests) * dests + me
         block = PAD + lax.div(g, LANE // dests) * slots
         count = counts[0, origin]
-        for k in range(0, slots, 2):
+        for k0 in range(0, slots, 4):
             ats, adds = [], []
-            for m in range(k, k + 2):
+            for m in range(k0, k0 + 4):
                 place = places[origin, m]
                 lane = place & (LANE - 1)
                 value = pltpu.roll(ref[pl.ds(block + m, 1), :], (lane - lane_in) & (LANE - 1), 1)
                 ats.append(place >> 7)
                 adds.append(jnp.where(lanes == jnp.where(m < count, lane, LANE), value, 0.0))
             olds = [tile[pl.ds(at, 1), :] for at in ats]
-            also = jnp.where(ats[0] == ats[1], adds[0], 0.0)
-            tile[pl.ds(ats[0], 1), :] = olds[0] + adds[0]
-            tile[pl.ds(ats[1], 1), :] = olds[1] + adds[1] + also
+            for k, (at, total) in enumerate(zip(ats, olds)):
+                total = total + adds[k]
+                for j in range(k):
+                    total = total + jnp.where(ats[j] == at, adds[j], 0.0)
+                tile[pl.ds(at, 1), :] = total
         return carry
 
-    lax.fori_loop(0, half, functools.partial(source, 0, mine), 0)
-    lax.fori_loop(0, half, functools.partial(source, 3, theirs), 0)
+    def both(n, carry):
+        source(0, mine, n, carry)
+        return source(3, theirs, n, carry)
+
+    lax.fori_loop(0, half, both, 0)
 
 
 def observe(row, column, places, counts, seen, tile, dests, across):
@@ -849,14 +870,17 @@
     forcing = obs_forcing[0, 0]
     dests = forcing.shape[1]
     counts = obs_count.reshape(1, -1)
-    line = [forcing, *(swapped(forcing, "tx", n) for n in range(1, min(across, 4)))]
+    other = swapped(forcing, "tx", 1)
+    pair = stacked(forcing, other)
+    tx = column.reshape(1)
+    *x_sent, ahead = x_edges(tx, state5, mask)
+    ahead = ahead.reshape(-1, LANE)
+    pair, *x_sent = lax.optimization_barrier((pair, *x_sent))
+    x_halos = from_neighbours(*x_sent, "tx")
+    line = [forcing, other, swapped(pair, "tx", 2)]
     for n in range(2, across.bit_length() - 1):
         blocks = jnp.concatenate(line)
         line = [blocks, swapped(blocks, "tx", 1 << n)]
-    tx = column.reshape(1)
-    *x_sent, ahead = x_edges(tx, state5, mask)
-    ahead = ahead.reshape(-1, LANE)
-    x_halos = from_neighbours(*x_sent, "tx")
     masked, matrices, parcel, in_sent, places = front(
         is_child, state2, mask, kappa, nudging, mixing, nests, line, ahead,
         obs_cell[0, :, :, 0], dims,

time: 37.1 us -> 35.8 us (0.965)
  the two profiles are of different devices: /device:TPU:9 before, /device:TPU:0 now
where the time goes in v2:
time: 35.8 us; the launch traced here: 35.6 us
  Pallas kernels  20.9 us (58%)
  starting transfers between devices  12.7 us (35%)
  between operations  1.45 us (4%)
  waiting for transfers between devices  0.47 us (1%)
    ppermute x7, starting transfers between devices, swapped(): lax.ppermute(value, axis, [(i, i ^ mask) for i in range(lax.axis_size(axi...  12 us
    pallas_call x1, Pallas kernels, tile_of(): pl.pallas_call(functools.partial(tile_kernel, levels, peers), in_specs=[S...  5.44 us
    pallas_call x1, Pallas kernels, front(): pl.pallas_call(functools.partial(front_kernel, levels, bs, slots), in_spe...  4.9 us
    pallas_call x1, Pallas kernels, base_of(): pl.pallas_call(functools.partial(base_kernel, levels, bs), in_specs=[SMEM...  2.88 us
    pallas_call x1, Pallas kernels, finish(): pl.pallas_call(functools.partial(finish_kernel, levels), in_specs=[SMEM]...  2.61 us
    pallas_call x1, Pallas kernels, observe(): pl.pallas_call(functools.partial(observe_kernel, dests, across), in_specs...  2.13 us
    pallas_call x1, Pallas kernels, x_edges(): pl.pallas_call(x_edges_kernel, in_specs=[SMEM, HBM, HBM], out_specs=[VMEM...  1.69 us
    pallas_call x1, Pallas kernels, outer(): pl.pallas_call(functools.partial(outer_kernel, levels, peers), in_specs=[...  1.2 us
  transfers between devices with their start and end apart: 8, of which 2 were waited for; matrix products, arithmetic and copies ran while one was open for 0% of the time, Pallas kernels for 51%

profile of v2, /device:TPU:0, one launch (start us, length us, event | category | flops | bytes accessed | tf_op | source)
XLA Modules:
  0.0 35.6 jit_solution(15308168951631446245)
XLA Ops:
  0.0 3.0 %collective-permute-start = (f32[16,16]{1,0:T(8,128)}, f32[16,16]{1,0:T(8,128)S(1)}, u32[]{:S(2)}, u32[]{:S(2)}) collective-permute-start(f32[16,16]{1,0:T(8,128)} %bitcast.17), channel_id=1, source_target_pairs={{0,1},{1,0},{2,3},{3,2},{4,5},{5,4},{6,7},{7,6},{8,9},{9,8},{10,11... | collective-permute-start | bytes 3080 | tf_op jit(solution)/shard_map/ppermute | solution.py:838
  3.0 1.7 %x_edges.1 = (f32[5,50,1,384]{3,2,1,0:T(1,128)S(1)}, f32[5,50,1,384]{3,2,1,0:T(1,128)S(1)}, f32[50,12,1,384]{3,2,1,0:T(1,128)S(1)}) custom-call(s32[1]{0:T(128)} %bitcast.2.tx.column, f32[5,50,12,1,384]{4,3,2,1,0:T(1,128)} %bitcast.27, s32[12,1,384]{2,1,0:T(1,128)} %bitcast.21), custom_call_target="tpu_custom_call" | custom-call | flops 10000000000 | bytes 100000000 | tf_op jit(solution)/shard_map/x_edges/pallas_call | solution.py:65
  4.7 0.1 collective-permute-done.two.refs_1_
  4.9 3.0 %collective-permute-start.1 = (f32[32,16]{1,0:T(8,128)S(1)}, f32[32,16]{1,0:T(8,128)S(1)}, u32[]{:S(2)}, u32[]{:S(2)}) collective-permute-start(f32[32,16]{1,0:T(8,128)S(1)} %stacked.1), channel_id=1, source_target_pairs={{0,2},{1,3},{2,0},{3,1},{4,6},{5,7},{6,4},{7,5},{8,10},{9,11},{10,... | collective-permute-start | bytes 6152 | tf_op jit(solution)/shard_map/ppermute | solution.py:838
  9.2 1.6 %collective-permute-start.2 = (f32[5,50,1,384]{3,2,1,0:T(1,128)S(1)}, f32[5,50,1,384]{3,2,1,0:T(1,128)S(1)}, u32[]{:S(2)}, u32[]{:S(2)}) collective-permute-start(f32[5,50,1,384]{3,2,1,0:T(1,128)S(1)} %get-tuple-element.28), channel_id=1, source_target_pairs={{0,1},{1,0},{2,3},{3,2},{4,5},{5,4},{6,7},{7,6},{8,9},{9,8},{10,11... | collective-permute-start | bytes 1152008 | tf_op jit(solution)/shard_map/ppermute | solution.py:838
  10.8 0.7 %collective-permute-start.3 = (f32[5,50,1,384]{3,2,1,0:T(1,128)S(1)}, f32[5,50,1,384]{3,2,1,0:T(1,128)S(1)}, u32[]{:S(2)}, u32[]{:S(2)}) collective-permute-start(f32[5,50,1,384]{3,2,1,0:T(1,128)S(1)} %get-tuple-element.29), channel_id=1, source_target_pairs={{1,2},{2,1},{5,6},{6,5},{9,10},{10,9},{13,14},{14,13},{17,18},{18,... | collective-permute-start | bytes 1152008 | tf_op jit(solution)/shard_map/ppermute | solution.py:834
  11.5 0.0 collective-permute-done.1.refs_2_
  11.5 0.0 copy-start
  11.6 0.0 copy-start.1
  11.6 4.9 %front.1 = (f32[5,12,56,384]{3,2,1,0:T(8,128)}, bf16[5,128,128]{2,1,0:T(8,128)(2,1)S(1)}, f32[72,128]{1,0:T(8,128)S(1)}, f32[500,128]{1,0:T(8,128)S(1)}, s32[16,16]{1,0:T(8,128)S(1)}) custom-call(s32[1]{0:T(128)} %bitcast.is_child, f32[9000,128]{1,0:T(8,128)} %bitcast.28, s32[12,1,384]{2,1,0:T(1,128)} %bitcast.22, f32[12,1,384]{2,1,0:T(1,128)} %bitcast.13, ...), custom_call_target="tpu_custom_call" | custom-call | flops 10000000000 | bytes 100000000 | tf_op jit(solution)/shard_map/front/pallas_call | solution.py:363
  16.5 0.1 collective-permute-start.4
  16.6 1.7 %collective-permute-start.6 = (f32[500,128]{1,0:T(8,128)S(1)}, f32[500,128]{1,0:T(8,128)S(1)}, u32[]{:S(2)}, u32[]{:S(2)}) collective-permute-start(f32[500,128]{1,0:T(8,128)S(1)} %get-tuple-element.37.in_sent), channel_id=1, source_target_pairs={{0,16},{16,0},{1,17},{17,1},{2,18},{18,2},{3,19},{19,3},{4,20},{20... | collective-permute-start | bytes 768008 | tf_op jit(solution)/shard_map/ppermute | solution.py:838
  18.3 0.1 repack.1.mine
  18.4 1.3 %collective-permute-start.5 = (f32[72,128]{1,0:T(8,128)S(1)}, f32[72,128]{1,0:T(8,128)S(1)}, u32[]{:S(2)}, u32[]{:S(2)}) collective-permute-start(f32[72,128]{1,0:T(8,128)S(1)} %repack.1.mine), channel_id=1, source_target_pairs={{0,12},{4,8},{8,4},{12,0},{1,13},{5,9},{9,5},{13,1},{2,14},{6,10},... | collective-permute-start | bytes 110600 | tf_op jit(solution)/shard_map/ppermute | solution.py:838
  19.6 0.0 collective-permute-done.2.x_first
  19.7 0.0 collective-permute-done.3.x_second
  19.7 2.9 %base.1 = f32[5,56,256]{2,1,0:T(8,128)S(1)} custom-call(s32[1]{0:T(128)} %bitcast.is_child, s32[1]{0:T(128)S(6)} %copy.15.nest_x, s32[1]{0:T(128)S(6)} %copy.16.nest_y, f32[5,12,56,384]{3,2,1,0:T(8,128)} %get-tuple-element.35.masked_in, bf16[5,128,128]{2,1,0:T(8,128)(2,1)S(1)} %get-tuple-element.32.matrices, f32[12,1,384]{2,1,0:T(1,128)S(1)} %bitcast.14, ...), custom_call_target="tpu_custom_call" | custom-call | flops 10000000000 | bytes 100000000 | tf_op jit(solution)/shard_map/base/pallas_call | solution.py:446
  22.6 0.0 copy-start.4
  22.6 1.2 %outer.1 = (f32[560,128]{1,0:T(8,128)S(1)}, f32[1800,128]{1,0:T(8,128)S(1)}) custom-call(s32[1]{0:T(128)} %bitcast.is_child, s32[1]{0:T(128)} %bitcast.2.tx.column, s32[1]{0:T(128)} %bitcast.1.ty.row, f32[9000,128]{1,0:T(8,128)} %bitcast.29, bf16[5,128,128]{2,1,0:T(8,128)(2,1)S(1)} %get-tuple-element.32.matrices, f32[5,56,256]{2,1,0:T(8,128)S(1)} %base.1, ...), custom_call_target="tpu_custom_call" | custom-call | tf_op jit(solution)/shard_map/outer/pallas_call | solution.py:591
  23.8 1.2 %collective-permute-start.7 = (f32[560,128]{1,0:T(8,128)S(1)}, f32[560,128]{1,0:T(8,128)S(1)}, u32[]{:S(2)}, u32[]{:S(2)}) collective-permute-start(f32[560,128]{1,0:T(8,128)S(1)} %get-tuple-element.38.out_sent), channel_id=1, source_target_pairs={{0,16},{16,0},{1,17},{17,1},{2,18},{18,2},{3,19},{19,3},{4,20},{20... | collective-permute-start | bytes 860168 | tf_op jit(solution)/shard_map/ppermute | solution.py:838
  25.0 5.4 %tile.1._ = f32[10080,128]{1,0:T(8,128)S(1)} custom-call(s32[1]{0:T(128)} %bitcast.2.tx.column, s32[1]{0:T(128)} %bitcast.1.ty.row, f32[9000,128]{1,0:T(8,128)} %bitcast.30, s32[12,1,384]{2,1,0:T(1,128)S(1)} %bitcast.23, bf16[5,128,128]{2,1,0:T(8,128)(2,1)S(1)} %get-tuple-element.32.matrices, f32[12,1,384]{2,1,0:T(1,128)S(1)} %bitcast.16, ...), custom_call_target="tpu_custom_call" | custom-call | flops 10000000000 | bytes 100000000 | tf_op jit(solution)/shard_map/tile/pallas_call | solution.py:659
  30.5 2.1 %observe.1.tile = f32[10080,128]{1,0:T(8,128)S(1)} custom-call(s32[1]{0:T(128)} %bitcast.1.ty.row, s32[1]{0:T(128)} %bitcast.2.tx.column, s32[1,16]{1,0:T(1,128)S(1)} %bitcast.20, s32[16,16]{1,0:T(8,128)S(1)} %get-tuple-element.26.places, f32[72,128]{1,0:T(8,128)S(1)} %repack.1.mine, ...), custom_call_target="tpu_custom_call", output_to_operand_aliasing={{}: (6, {})} | custom-call | tf_op jit(solution)/shard_map/observe/pallas_call | solution.py:714
  32.6 0.3 collective-permute-done.7.out_arrived
  32.9 2.6 %finish.1 = f32[9000,128]{1,0:T(8,128)} custom-call(s32[1]{0:T(128)} %bitcast.is_child, s32[1]{0:T(128)S(6)} %copy.15.nest_x, s32[1]{0:T(128)S(6)} %copy.16.nest_y, f32[10080,128]{1,0:T(8,128)S(1)} %observe.1.tile, s32[12,1,384]{2,1,0:T(1,128)S(1)} %bitcast.24, f32[500,128]{1,0:T(8,128)S(1)} %collective-permute-done.6.in_arrived, ...), custom_call_target="tpu_custom_call" | custom-call | flops 10000000000 | bytes 100000000 | tf_op jit(solution)/shard_map/finish/pallas_call | solution.py:814
  (13 shorter events, 0.0 us)
Async XLA Ops:
  0.0 4.9 %collective-permute-start = (f32[16,16]{1,0:T(8,128)}, f32[16,16]{1,0:T(8,128)S(1)}, u32[]{:S(2)}, u32[]{:S(2)}) collective-permute-start(f32[16,16]{1,0:T(8,128)} %bitcast.17), channel_id=1, source_target_pairs={{0,1},{1,0},{2,3},{3,2},{4,5},{5,4},{6,7},{7,6},{8,9},{9,8},{10,11... | collective-permute-start | bytes 3080 | tf_op jit(solution)/shard_map/ppermute | solution.py:838
  3.0 1.8 %copy-start.2 = (f32[1,1,16,16]{3,2,1,0:T(8,128)S(1)}, f32[1,1,16,16]{3,2,1,0:T(8,128)}, u32[]{:S(2)}) copy-start(f32[1,1,16,16]{3,2,1,0:T(8,128)} %param.17) | copy-start | bytes 3076
  3.0 8.5 %copy-start.5 = (s32[1,16,16,1]{2,3,1,0:T(1,128)S(1)}, s32[1,16,16,1]{2,3,1,0:T(1,128)}, u32[]{:S(2)}) copy-start(s32[1,16,16,1]{2,3,1,0:T(1,128)} %param.18) | copy-start | bytes 3076
  4.9 6.7 %collective-permute-start.1 = (f32[32,16]{1,0:T(8,128)S(1)}, f32[32,16]{1,0:T(8,128)S(1)}, u32[]{:S(2)}, u32[]{:S(2)}) collective-permute-start(f32[32,16]{1,0:T(8,128)S(1)} %stacked.1), channel_id=1, source_target_pairs={{0,2},{1,3},{2,0},{3,1},{4,6},{5,7},{6,4},{7,5},{8,10},{9,11},{10,... | collective-permute-start | bytes 6152 | tf_op jit(solution)/shard_map/ppermute | solution.py:838
  9.2 10.4 %collective-permute-start.2 = (f32[5,50,1,384]{3,2,1,0:T(1,128)S(1)}, f32[5,50,1,384]{3,2,1,0:T(1,128)S(1)}, u32[]{:S(2)}, u32[]{:S(2)}) collective-permute-start(f32[5,50,1,384]{3,2,1,0:T(1,128)S(1)} %get-tuple-element.28), channel_id=1, source_target_pairs={{0,1},{1,0},{2,3},{3,2},{4,5},{5,4},{6,7},{7,6},{8,9},{9,8},{10,11... | collective-permute-start | bytes 1152008 | tf_op jit(solution)/shard_map/ppermute | solution.py:838
  10.8 8.8 %collective-permute-start.3 = (f32[5,50,1,384]{3,2,1,0:T(1,128)S(1)}, f32[5,50,1,384]{3,2,1,0:T(1,128)S(1)}, u32[]{:S(2)}, u32[]{:S(2)}) collective-permute-start(f32[5,50,1,384]{3,2,1,0:T(1,128)S(1)} %get-tuple-element.29), channel_id=1, source_target_pairs={{1,2},{2,1},{5,6},{6,5},{9,10},{10,9},{13,14},{14,13},{17,18},{18,... | collective-permute-start | bytes 1152008 | tf_op jit(solution)/shard_map/ppermute | solution.py:834
  11.5 8.1 %copy-start = (f32[12,384]{1,0:T(8,128)S(1)}, f32[12,384]{1,0:T(8,128)}, u32[]{:S(2)}) copy-start(f32[12,384]{1,0:T(8,128)} %nudging.5) | copy-start | bytes 55300
  11.6 8.1 %copy-start.1 = (f32[1,12,384]{2,0,1:T(1,128)S(1)}, f32[1,12,384]{2,0,1:T(1,128)}, u32[]{:S(2)}) copy-start(f32[1,12,384]{2,0,1:T(1,128)} %param.12) | copy-start | bytes 55300
  16.5 1.8 %collective-permute-start.4 = (f32[72,128]{1,0:T(8,128)S(1)}, f32[72,128]{1,0:T(8,128)S(1)}, u32[]{:S(2)}, u32[]{:S(2)}) collective-permute-start(f32[72,128]{1,0:T(8,128)S(1)} %get-tuple-element.30.parcel), channel_id=1, source_target_pairs={{0,4},{4,0},{8,12},{12,8},{1,5},{5,1},{9,13},{13,9},{2,6},{6,2},{1... | collective-permute-start | bytes 110600 | tf_op jit(solution)/shard_map/ppermute | solution.py:838
  16.6 16.1 %collective-permute-start.6 = (f32[500,128]{1,0:T(8,128)S(1)}, f32[500,128]{1,0:T(8,128)S(1)}, u32[]{:S(2)}, u32[]{:S(2)}) collective-permute-start(f32[500,128]{1,0:T(8,128)S(1)} %get-tuple-element.37.in_sent), channel_id=1, source_target_pairs={{0,16},{16,0},{1,17},{17,1},{2,18},{18,2},{3,19},{19,3},{4,20},{20... | collective-permute-start | bytes 768008 | tf_op jit(solution)/shard_map/ppermute | solution.py:838
  18.4 4.2 %collective-permute-start.5 = (f32[72,128]{1,0:T(8,128)S(1)}, f32[72,128]{1,0:T(8,128)S(1)}, u32[]{:S(2)}, u32[]{:S(2)}) collective-permute-start(f32[72,128]{1,0:T(8,128)S(1)} %repack.1.mine), channel_id=1, source_target_pairs={{0,12},{4,8},{8,4},{12,0},{1,13},{5,9},{9,5},{13,1},{2,14},{6,10},... | collective-permute-start | bytes 110600 | tf_op jit(solution)/shard_map/ppermute | solution.py:838
  22.6 2.5 %copy-start.4 = (s32[1,12,384]{2,0,1:T(1,128)S(1)}, s32[1,12,384]{2,0,1:T(1,128)}, u32[]{:S(2)}) copy-start(s32[1,12,384]{2,0,1:T(1,128)} %param.11) | copy-start | bytes 55300
  23.8 9.2 %collective-permute-start.7 = (f32[560,128]{1,0:T(8,128)S(1)}, f32[560,128]{1,0:T(8,128)S(1)}, u32[]{:S(2)}, u32[]{:S(2)}) collective-permute-start(f32[560,128]{1,0:T(8,128)S(1)} %get-tuple-element.38.out_sent), channel_id=1, source_target_pairs={{0,16},{16,0},{1,17},{17,1},{2,18},{18,2},{3,19},{19,3},{4,20},{20... | collective-permute-start | bytes 860168 | tf_op jit(solution)/shard_map/ppermute | solution.py:838
  25.0 5.5 %copy-start.3 = (s32[1,16,1]{1,2,0:T(1,128)S(1)}, s32[1,16,1]{1,2,0:T(1,128)}, u32[]{:S(2)}) copy-start(s32[1,16,1]{1,2,0:T(1,128)} %param.19) | copy-start | bytes 196

commit v3 on v2

--- a/solution.py
+++ b/solution.py
@@ -38,7 +38,7 @@
     return pltpu.with_memory_space_constraint(value, pltpu.VMEM)
 
 
-def x_edges_kernel(tx, state, mask, first, second, ahead, buf, mask_buf, sems):
+def x_edges_kernel(tx, _, __, state, mask, first, second, ahead, buf, mask_buf, sems):
     fields, _, cols = state.shape[:3]
     even = lax.rem(tx[0], 2) == 0
     ends = (jnp.where(even, cols - 1, 0), jnp.where(even, 0, cols - 1))
@@ -59,12 +59,12 @@
     copies[-1].wait()
 
 
-def x_edges(tx, state5, mask):
+def x_edges(tx, nests, state5, mask):
     fields, levels, cols, _, rows = state5.shape
     edge = (fields, levels, 1, rows)
     return pl.pallas_call(
         x_edges_kernel,
-        in_specs=[SMEM, HBM, HBM],
+        in_specs=[SMEM] * 3 + [HBM] * 2,
         out_specs=[VMEM] * 3,
         out_shape=[pltpu.VMEM(edge, F32)] * 2 + [pltpu.VMEM(state5.shape[1:], F32)],
         scratch_shapes=[
@@ -75,7 +75,7 @@
         compiler_params=pltpu.CompilerParams(vmem_limit_bytes=8 * MIB),
         cost_estimate=COST,
         name="x_edges",
-    )(tx, in_hbm(state5), in_hbm(mask))
+    )(tx, *nests, in_hbm(state5), in_hbm(mask))
 
 
 def x_halos_of(tx, first, second, f):
@@ -873,7 +873,7 @@
     other = swapped(forcing, "tx", 1)
     pair = stacked(forcing, other)
     tx = column.reshape(1)
-    *x_sent, ahead = x_edges(tx, state5, mask)
+    *x_sent, ahead = x_edges(tx, nests, state5, mask)
     ahead = ahead.reshape(-1, LANE)
     pair, *x_sent = lax.optimization_barrier((pair, *x_sent))
     x_halos = from_neighbours(*x_sent, "tx")

time: 35.8 us -> 35.6 us (level); the launches traced: 35.6 us -> 34.9 us
  starting transfers between devices: 12.7 us -> 11.8 us
    ppermute x7, starting transfers between devices: 12 us -> 11.1 us  [swapped(): lax.ppermute(value, axis, [(i, i ^ mask) for i in range(lax.axis_size(axi...]
  transfers between devices with their start and end apart: 8 -> 8, of which waited for: 2 -> 1; matrix products, arithmetic and copies ran while one was open for 0% -> 0% of each run, Pallas kernels for 51% -> 52%
where the time goes in v3:
time: 35.6 us; the launch traced here: 34.9 us
  Pallas kernels  20.9 us (59%)
  starting transfers between devices  11.8 us (33%)
  between operations  1.46 us (4%)
  waiting for transfers between devices  0.75 us (2%)
    ppermute x7, starting transfers between devices, swapped(): lax.ppermute(value, axis, [(i, i ^ mask) for i in range(lax.axis_size(axi...  11.1 us
    pallas_call x1, Pallas kernels, tile_of(): pl.pallas_call(functools.partial(tile_kernel, levels, peers), in_specs=[S...  5.44 us
    pallas_call x1, Pallas kernels, front(): pl.pallas_call(functools.partial(front_kernel, levels, bs, slots), in_spe...  4.91 us
    pallas_call x1, Pallas kernels, base_of(): pl.pallas_call(functools.partial(base_kernel, levels, bs), in_specs=[SMEM...  2.88 us
    pallas_call x1, Pallas kernels, finish(): pl.pallas_call(functools.partial(finish_kernel, levels), in_specs=[SMEM]...  2.61 us
    pallas_call x1, Pallas kernels, observe(): pl.pallas_call(functools.partial(observe_kernel, dests, across), in_specs...  2.13 us
    pallas_call x1, Pallas kernels, x_edges(): pl.pallas_call(x_edges_kernel, in_specs=[SMEM] * 3 + [HBM] * 2, out_specs...  1.69 us
    pallas_call x1, Pallas kernels, outer(): pl.pallas_call(functools.partial(outer_kernel, levels, peers), in_specs=[...  1.2 us
  transfers between devices with their start and end apart: 8, of which 1 were waited for; matrix products, arithmetic and copies ran while one was open for 0% of the time, Pallas kernels for 52%

profile of v3, /device:TPU:0, one launch (start us, length us, event | category | flops | bytes accessed | tf_op | source)
XLA Modules:
  0.0 34.9 jit_solution(635263729047477643)
XLA Ops:
  0.0 3.0 %collective-permute-start = (f32[16,16]{1,0:T(8,128)}, f32[16,16]{1,0:T(8,128)S(1)}, u32[]{:S(2)}, u32[]{:S(2)}) collective-permute-start(f32[16,16]{1,0:T(8,128)} %bitcast.17), channel_id=1, source_target_pairs={{0,1},{1,0},{2,3},{3,2},{4,5},{5,4},{6,7},{7,6},{8,9},{9,8},{10,11... | collective-permute-start | bytes 3080 | tf_op jit(solution)/shard_map/ppermute | solution.py:838
  4.3 1.7 %x_edges.1 = (f32[5,50,1,384]{3,2,1,0:T(1,128)S(1)}, f32[5,50,1,384]{3,2,1,0:T(1,128)S(1)}, f32[50,12,1,384]{3,2,1,0:T(1,128)S(1)}) custom-call(s32[1]{0:T(128)} %bitcast.2.tx.column, s32[1]{0:T(128)S(6)} %copy.15._.nest_x, s32[1]{0:T(128)S(6)} %copy.16.__.nest_y, f32[5,50,12,1,384]{4,3,2,1,0:T(1,128)} %bitcast.27, s32[12,1,384]{2,1,0:T(1,128)} %bitcast.21), custom_call_target="tpu_custom_call" | custom-call | flops 10000000000 | bytes 100000000 | tf_op jit(solution)/shard_map/x_edges/pallas_call | solution.py:65
  6.0 0.0 collective-permute-done.two.refs_1_
  6.1 2.7 %collective-permute-start.1 = (f32[32,16]{1,0:T(8,128)S(1)}, f32[32,16]{1,0:T(8,128)S(1)}, u32[]{:S(2)}, u32[]{:S(2)}) collective-permute-start(f32[32,16]{1,0:T(8,128)S(1)} %stacked.1), channel_id=1, source_target_pairs={{0,2},{1,3},{2,0},{3,1},{4,6},{5,7},{6,4},{7,5},{8,10},{9,11},{10,... | collective-permute-start | bytes 6152 | tf_op jit(solution)/shard_map/ppermute | solution.py:838
  8.7 0.8 %collective-permute-start.2 = (f32[5,50,1,384]{3,2,1,0:T(1,128)S(1)}, f32[5,50,1,384]{3,2,1,0:T(1,128)S(1)}, u32[]{:S(2)}, u32[]{:S(2)}) collective-permute-start(f32[5,50,1,384]{3,2,1,0:T(1,128)S(1)} %get-tuple-element.28), channel_id=1, source_target_pairs={{0,1},{1,0},{2,3},{3,2},{4,5},{5,4},{6,7},{7,6},{8,9},{9,8},{10,11... | collective-permute-start | bytes 1152008 | tf_op jit(solution)/shard_map/ppermute | solution.py:838
  9.5 0.7 %collective-permute-start.3 = (f32[5,50,1,384]{3,2,1,0:T(1,128)S(1)}, f32[5,50,1,384]{3,2,1,0:T(1,128)S(1)}, u32[]{:S(2)}, u32[]{:S(2)}) collective-permute-start(f32[5,50,1,384]{3,2,1,0:T(1,128)S(1)} %get-tuple-element.29), channel_id=1, source_target_pairs={{1,2},{2,1},{5,6},{6,5},{9,10},{10,9},{13,14},{14,13},{17,18},{18,... | collective-permute-start | bytes 1152008 | tf_op jit(solution)/shard_map/ppermute | solution.py:834
  10.2 0.7 %collective-permute-done.1.refs_2_ = f32[32,16]{1,0:T(8,128)S(1)} collective-permute-done((f32[32,16]{1,0:T(8,128)S(1)}, f32[32,16]{1,0:T(8,128)S(1)}, u32[]{:S(2)}, u32[]{:S(2)}) %collective-permute-start.1) | collective-permute-done | bytes 2080 | tf_op jit(solution)/shard_map/ppermute | solution.py:838
  10.9 4.9 %front.1 = (f32[5,12,56,384]{3,2,1,0:T(8,128)}, bf16[5,128,128]{2,1,0:T(8,128)(2,1)S(1)}, f32[72,128]{1,0:T(8,128)S(1)}, f32[500,128]{1,0:T(8,128)S(1)}, s32[16,16]{1,0:T(8,128)S(1)}) custom-call(s32[1]{0:T(128)} %bitcast.is_child, f32[9000,128]{1,0:T(8,128)} %bitcast.28, s32[12,1,384]{2,1,0:T(1,128)} %bitcast.22, f32[12,1,384]{2,1,0:T(1,128)} %bitcast.13, ...), custom_call_target="tpu_custom_call" | custom-call | flops 10000000000 | bytes 100000000 | tf_op jit(solution)/shard_map/front/pallas_call | solution.py:363
  15.8 0.1 collective-permute-start.4
  15.9 1.7 %collective-permute-start.6 = (f32[500,128]{1,0:T(8,128)S(1)}, f32[500,128]{1,0:T(8,128)S(1)}, u32[]{:S(2)}, u32[]{:S(2)}) collective-permute-start(f32[500,128]{1,0:T(8,128)S(1)} %get-tuple-element.37.in_sent), channel_id=1, source_target_pairs={{0,16},{16,0},{1,17},{17,1},{2,18},{18,2},{3,19},{19,3},{4,20},{20... | collective-permute-start | bytes 768008 | tf_op jit(solution)/shard_map/ppermute | solution.py:838
  17.6 0.0 collective-permute-done.4.arrived.first
  17.6 0.1 repack.1.mine
  17.7 1.3 %collective-permute-start.5 = (f32[72,128]{1,0:T(8,128)S(1)}, f32[72,128]{1,0:T(8,128)S(1)}, u32[]{:S(2)}, u32[]{:S(2)}) collective-permute-start(f32[72,128]{1,0:T(8,128)S(1)} %repack.1.mine), channel_id=1, source_target_pairs={{0,12},{4,8},{8,4},{12,0},{1,13},{5,9},{9,5},{13,1},{2,14},{6,10},... | collective-permute-start | bytes 110600 | tf_op jit(solution)/shard_map/ppermute | solution.py:838
  19.0 0.0 collective-permute-done.2.x_first
  19.0 0.0 collective-permute-done.3.x_second
  19.0 2.9 %base.1 = f32[5,56,256]{2,1,0:T(8,128)S(1)} custom-call(s32[1]{0:T(128)} %bitcast.is_child, s32[1]{0:T(128)S(6)} %copy.15._.nest_x, s32[1]{0:T(128)S(6)} %copy.16.__.nest_y, f32[5,12,56,384]{3,2,1,0:T(8,128)} %get-tuple-element.35.masked_in, bf16[5,128,128]{2,1,0:T(8,128)(2,1)S(1)} %get-tuple-element.32.matrices, f32[12,1,384]{2,1,0:T(1,128)S(1)} %bitcast.14, ...), custom_call_target="tpu_custom_call" | custom-call | flops 10000000000 | bytes 100000000 | tf_op jit(solution)/shard_map/base/pallas_call | solution.py:446
  21.9 0.0 copy-start.4
  21.9 0.0 collective-permute-done.5.second.theirs
  21.9 1.2 %outer.1 = (f32[560,128]{1,0:T(8,128)S(1)}, f32[1800,128]{1,0:T(8,128)S(1)}) custom-call(s32[1]{0:T(128)} %bitcast.is_child, s32[1]{0:T(128)} %bitcast.2.tx.column, s32[1]{0:T(128)} %bitcast.1.ty.row, f32[9000,128]{1,0:T(8,128)} %bitcast.29, bf16[5,128,128]{2,1,0:T(8,128)(2,1)S(1)} %get-tuple-element.32.matrices, f32[5,56,256]{2,1,0:T(8,128)S(1)} %base.1, ...), custom_call_target="tpu_custom_call" | custom-call | tf_op jit(solution)/shard_map/outer/pallas_call | solution.py:591
  23.1 1.6 %collective-permute-start.7 = (f32[560,128]{1,0:T(8,128)S(1)}, f32[560,128]{1,0:T(8,128)S(1)}, u32[]{:S(2)}, u32[]{:S(2)}) collective-permute-start(f32[560,128]{1,0:T(8,128)S(1)} %get-tuple-element.38.out_sent), channel_id=1, source_target_pairs={{0,16},{16,0},{1,17},{17,1},{2,18},{18,2},{3,19},{19,3},{4,20},{20... | collective-permute-start | bytes 860168 | tf_op jit(solution)/shard_map/ppermute | solution.py:838
  24.7 5.4 %tile.1._ = f32[10080,128]{1,0:T(8,128)S(1)} custom-call(s32[1]{0:T(128)} %bitcast.2.tx.column, s32[1]{0:T(128)} %bitcast.1.ty.row, f32[9000,128]{1,0:T(8,128)} %bitcast.30, s32[12,1,384]{2,1,0:T(1,128)S(1)} %bitcast.23, bf16[5,128,128]{2,1,0:T(8,128)(2,1)S(1)} %get-tuple-element.32.matrices, f32[12,1,384]{2,1,0:T(1,128)S(1)} %bitcast.16, ...), custom_call_target="tpu_custom_call" | custom-call | flops 10000000000 | bytes 100000000 | tf_op jit(solution)/shard_map/tile/pallas_call | solution.py:659
  30.2 2.1 %observe.1.tile = f32[10080,128]{1,0:T(8,128)S(1)} custom-call(s32[1]{0:T(128)} %bitcast.1.ty.row, s32[1]{0:T(128)} %bitcast.2.tx.column, s32[1,16]{1,0:T(1,128)S(1)} %bitcast.20, s32[16,16]{1,0:T(8,128)S(1)} %get-tuple-element.26.places, f32[72,128]{1,0:T(8,128)S(1)} %repack.1.mine, ...), custom_call_target="tpu_custom_call", output_to_operand_aliasing={{}: (6, {})} | custom-call | tf_op jit(solution)/shard_map/observe/pallas_call | solution.py:714
  32.3 0.0 collective-permute-done.7.out_arrived
  32.3 2.6 %finish.1 = f32[9000,128]{1,0:T(8,128)} custom-call(s32[1]{0:T(128)} %bitcast.is_child, s32[1]{0:T(128)S(6)} %copy.15._.nest_x, s32[1]{0:T(128)S(6)} %copy.16.__.nest_y, f32[10080,128]{1,0:T(8,128)S(1)} %observe.1.tile, s32[12,1,384]{2,1,0:T(1,128)S(1)} %bitcast.24, f32[500,128]{1,0:T(8,128)S(1)} %collective-permute-done.6.in_arrived, ...), custom_call_target="tpu_custom_call" | custom-call | flops 10000000000 | bytes 100000000 | tf_op jit(solution)/shard_map/finish/pallas_call | solution.py:814
  (13 shorter events, 0.0 us)
Async XLA Ops:
  0.0 6.0 %collective-permute-start = (f32[16,16]{1,0:T(8,128)}, f32[16,16]{1,0:T(8,128)S(1)}, u32[]{:S(2)}, u32[]{:S(2)}) collective-permute-start(f32[16,16]{1,0:T(8,128)} %bitcast.17), channel_id=1, source_target_pairs={{0,1},{1,0},{2,3},{3,2},{4,5},{5,4},{6,7},{7,6},{8,9},{9,8},{10,11... | collective-permute-start | bytes 3080 | tf_op jit(solution)/shard_map/ppermute | solution.py:838
  4.3 1.7 %copy-start.2 = (f32[1,1,16,16]{3,2,1,0:T(8,128)S(1)}, f32[1,1,16,16]{3,2,1,0:T(8,128)}, u32[]{:S(2)}) copy-start(f32[1,1,16,16]{3,2,1,0:T(8,128)} %param.17) | copy-start | bytes 3076
  4.3 6.5 %copy-start.5 = (s32[1,16,16,1]{2,3,1,0:T(1,128)S(1)}, s32[1,16,16,1]{2,3,1,0:T(1,128)}, u32[]{:S(2)}) copy-start(s32[1,16,16,1]{2,3,1,0:T(1,128)} %param.18) | copy-start | bytes 3076
  6.1 4.8 %collective-permute-start.1 = (f32[32,16]{1,0:T(8,128)S(1)}, f32[32,16]{1,0:T(8,128)S(1)}, u32[]{:S(2)}, u32[]{:S(2)}) collective-permute-start(f32[32,16]{1,0:T(8,128)S(1)} %stacked.1), channel_id=1, source_target_pairs={{0,2},{1,3},{2,0},{3,1},{4,6},{5,7},{6,4},{7,5},{8,10},{9,11},{10,... | collective-permute-start | bytes 6152 | tf_op jit(solution)/shard_map/ppermute | solution.py:838
  8.7 10.3 %collective-permute-start.2 = (f32[5,50,1,384]{3,2,1,0:T(1,128)S(1)}, f32[5,50,1,384]{3,2,1,0:T(1,128)S(1)}, u32[]{:S(2)}, u32[]{:S(2)}) collective-permute-start(f32[5,50,1,384]{3,2,1,0:T(1,128)S(1)} %get-tuple-element.28), channel_id=1, source_target_pairs={{0,1},{1,0},{2,3},{3,2},{4,5},{5,4},{6,7},{7,6},{8,9},{9,8},{10,11... | collective-permute-start | bytes 1152008 | tf_op jit(solution)/shard_map/ppermute | solution.py:838
  9.5 9.5 %collective-permute-start.3 = (f32[5,50,1,384]{3,2,1,0:T(1,128)S(1)}, f32[5,50,1,384]{3,2,1,0:T(1,128)S(1)}, u32[]{:S(2)}, u32[]{:S(2)}) collective-permute-start(f32[5,50,1,384]{3,2,1,0:T(1,128)S(1)} %get-tuple-element.29), channel_id=1, source_target_pairs={{1,2},{2,1},{5,6},{6,5},{9,10},{10,9},{13,14},{14,13},{17,18},{18,... | collective-permute-start | bytes 1152008 | tf_op jit(solution)/shard_map/ppermute | solution.py:834
  10.9 8.1 %copy-start = (f32[12,384]{1,0:T(8,128)S(1)}, f32[12,384]{1,0:T(8,128)}, u32[]{:S(2)}) copy-start(f32[12,384]{1,0:T(8,128)} %nudging.5) | copy-start | bytes 55300
  10.9 8.1 %copy-start.1 = (f32[1,12,384]{2,0,1:T(1,128)S(1)}, f32[1,12,384]{2,0,1:T(1,128)}, u32[]{:S(2)}) copy-start(f32[1,12,384]{2,0,1:T(1,128)} %param.12) | copy-start | bytes 55300
  15.8 1.8 %collective-permute-start.4 = (f32[72,128]{1,0:T(8,128)S(1)}, f32[72,128]{1,0:T(8,128)S(1)}, u32[]{:S(2)}, u32[]{:S(2)}) collective-permute-start(f32[72,128]{1,0:T(8,128)S(1)} %get-tuple-element.30.parcel), channel_id=1, source_target_pairs={{0,4},{4,0},{8,12},{12,8},{1,5},{5,1},{9,13},{13,9},{2,6},{6,2},{1... | collective-permute-start | bytes 110600 | tf_op jit(solution)/shard_map/ppermute | solution.py:838
  15.9 16.4 %collective-permute-start.6 = (f32[500,128]{1,0:T(8,128)S(1)}, f32[500,128]{1,0:T(8,128)S(1)}, u32[]{:S(2)}, u32[]{:S(2)}) collective-permute-start(f32[500,128]{1,0:T(8,128)S(1)} %get-tuple-element.37.in_sent), channel_id=1, source_target_pairs={{0,16},{16,0},{1,17},{17,1},{2,18},{18,2},{3,19},{19,3},{4,20},{20... | collective-permute-start | bytes 768008 | tf_op jit(solution)/shard_map/ppermute | solution.py:838
  17.7 4.2 %collective-permute-start.5 = (f32[72,128]{1,0:T(8,128)S(1)}, f32[72,128]{1,0:T(8,128)S(1)}, u32[]{:S(2)}, u32[]{:S(2)}) collective-permute-start(f32[72,128]{1,0:T(8,128)S(1)} %repack.1.mine), channel_id=1, source_target_pairs={{0,12},{4,8},{8,4},{12,0},{1,13},{5,9},{9,5},{13,1},{2,14},{6,10},... | collective-permute-start | bytes 110600 | tf_op jit(solution)/shard_map/ppermute | solution.py:838
  21.9 2.8 %copy-start.4 = (s32[1,12,384]{2,0,1:T(1,128)S(1)}, s32[1,12,384]{2,0,1:T(1,128)}, u32[]{:S(2)}) copy-start(s32[1,12,384]{2,0,1:T(1,128)} %param.11) | copy-start | bytes 55300
  23.1 9.2 %collective-permute-start.7 = (f32[560,128]{1,0:T(8,128)S(1)}, f32[560,128]{1,0:T(8,128)S(1)}, u32[]{:S(2)}, u32[]{:S(2)}) collective-permute-start(f32[560,128]{1,0:T(8,128)S(1)} %get-tuple-element.38.out_sent), channel_id=1, source_target_pairs={{0,16},{16,0},{1,17},{17,1},{2,18},{18,2},{3,19},{19,3},{4,20},{20... | collective-permute-start | bytes 860168 | tf_op jit(solution)/shard_map/ppermute | solution.py:838
  24.7 5.5 %copy-start.3 = (s32[1,16,1]{1,2,0:T(1,128)S(1)}, s32[1,16,1]{1,2,0:T(1,128)}, u32[]{:S(2)}) copy-start(s32[1,16,1]{1,2,0:T(1,128)} %param.19) | copy-start | bytes 196

commit v4 on v3

--- a/solution.py
+++ b/solution.py
@@ -332,7 +332,7 @@
         return total_edges + pltpu.roll(own_edges, 2 * f * cols, 1)
 
     own_edges = field(0, jnp.zeros((PAD, LANE), F32), first=True)
-    parcel[:PAD, :] = lax.fori_loop(1, fields, field, own_edges)
+    parcel[:PAD, :] = lax.fori_loop(1, fields, field, own_edges, unroll=True)
     parcel[PAD:, :] = jnp.zeros((parcel.shape[0] - PAD, LANE), F32)
     lane = 0
     for blocks in line:
@@ -419,7 +419,7 @@
             child_rows(f, bs, masked, weights, wide)
             return carry
 
-        lax.fori_loop(0, fields, field, 0)
+        lax.fori_loop(0, fields, field, 0, unroll=True)
 
     @pl.when(is_child[0] == 0)
     def _():
@@ -431,7 +431,7 @@
             parent_rows(f, bs, nest_x, nest_y, masked, kappa, stack)
             return carry
 
-        lax.fori_loop(0, fields, field, 0)
+        lax.fori_loop(0, fields, field, 0, unroll=True)
 
     def emit(f, mixed):
         base[f, :, :] = mixed[:PAD, :]
@@ -650,7 +650,7 @@
         return carry
 
     field(0, 0, leading=True)
-    lax.fori_loop(1, fields, field, 0)
+    lax.fori_loop(1, fields, field, 0, unroll=True)
 
 
 def tile_of(tx, ty, state2, mask, matrices, kappa, x_halos, firsts, ahead, dims, peers):

time: 35.6 us -> 36.5 us (1.025)
  Pallas kernels: 20.9 us -> 21.5 us
    pallas_call x1, Pallas kernels: 5.44 us -> 6.21 us  [tile_of(): pl.pallas_call(functools.partial(tile_kernel, levels, peers), in_specs=[S...]
  transfers between devices with their start and end apart: 8 -> 8, of which waited for: 1 -> 2; matrix products, arithmetic and copies ran while one was open for 0% -> 0% of each run, Pallas kernels for 52% -> 53%
where the time goes in v4:
time: 36.5 us; the launch traced here: 35.9 us
  Pallas kernels  21.5 us (59%)
  starting transfers between devices  11.8 us (32%)
  between operations  1.62 us (4%)
  waiting for transfers between devices  0.98 us (3%)
    ppermute x7, starting transfers between devices, swapped(): lax.ppermute(value, axis, [(i, i ^ mask) for i in range(lax.axis_size(axi...  11.1 us
    pallas_call x1, Pallas kernels, tile_of(): pl.pallas_call(functools.partial(tile_kernel, levels, peers), in_specs=[S...  6.21 us
    pallas_call x1, Pallas kernels, front(): pl.pallas_call(functools.partial(front_kernel, levels, bs, slots), in_spe...  4.55 us
    pallas_call x1, Pallas kernels, base_of(): pl.pallas_call(functools.partial(base_kernel, levels, bs), in_specs=[SMEM...  2.85 us
    pallas_call x1, Pallas kernels, finish(): pl.pallas_call(functools.partial(finish_kernel, levels), in_specs=[SMEM]...  2.61 us
    pallas_call x1, Pallas kernels, observe(): pl.pallas_call(functools.partial(observe_kernel, dests, across), in_specs...  2.13 us
    pallas_call x1, Pallas kernels, x_edges(): pl.pallas_call(x_edges_kernel, in_specs=[SMEM] * 3 + [HBM] * 2, out_specs...  1.69 us
    pallas_call x1, Pallas kernels, outer(): pl.pallas_call(functools.partial(outer_kernel, levels, peers), in_specs=[...  1.37 us
  transfers between devices with their start and end apart: 8, of which 2 were waited for; matrix products, arithmetic and copies ran while one was open for 0% of the time, Pallas kernels for 53%

profile of v4, /device:TPU:0, one launch (start us, length us, event | category | flops | bytes accessed | tf_op | source)
XLA Modules:
  0.0 35.9 jit_solution(16217320471145391707)
XLA Ops:
  0.0 3.0 %collective-permute-start = (f32[16,16]{1,0:T(8,128)}, f32[16,16]{1,0:T(8,128)S(1)}, u32[]{:S(2)}, u32[]{:S(2)}) collective-permute-start(f32[16,16]{1,0:T(8,128)} %bitcast.17), channel_id=1, source_target_pairs={{0,1},{1,0},{2,3},{3,2},{4,5},{5,4},{6,7},{7,6},{8,9},{9,8},{10,11... | collective-permute-start | bytes 3080 | tf_op jit(solution)/shard_map/ppermute | solution.py:838
  4.3 1.7 %x_edges.1 = (f32[5,50,1,384]{3,2,1,0:T(1,128)S(1)}, f32[5,50,1,384]{3,2,1,0:T(1,128)S(1)}, f32[50,12,1,384]{3,2,1,0:T(1,128)S(1)}) custom-call(s32[1]{0:T(128)} %bitcast.2.tx.column, s32[1]{0:T(128)S(6)} %copy.15._.nest_x, s32[1]{0:T(128)S(6)} %copy.16.__.nest_y, f32[5,50,12,1,384]{4,3,2,1,0:T(1,128)} %bitcast.27, s32[12,1,384]{2,1,0:T(1,128)} %bitcast.21), custom_call_target="tpu_custom_call" | custom-call | flops 10000000000 | bytes 100000000 | tf_op jit(solution)/shard_map/x_edges/pallas_call | solution.py:65
  6.0 0.0 collective-permute-done.two.refs_1_
  6.1 2.7 %collective-permute-start.1 = (f32[32,16]{1,0:T(8,128)S(1)}, f32[32,16]{1,0:T(8,128)S(1)}, u32[]{:S(2)}, u32[]{:S(2)}) collective-permute-start(f32[32,16]{1,0:T(8,128)S(1)} %stacked.1), channel_id=1, source_target_pairs={{0,2},{1,3},{2,0},{3,1},{4,6},{5,7},{6,4},{7,5},{8,10},{9,11},{10,... | collective-permute-start | bytes 6152 | tf_op jit(solution)/shard_map/ppermute | solution.py:838
  8.7 0.8 %collective-permute-start.2 = (f32[5,50,1,384]{3,2,1,0:T(1,128)S(1)}, f32[5,50,1,384]{3,2,1,0:T(1,128)S(1)}, u32[]{:S(2)}, u32[]{:S(2)}) collective-permute-start(f32[5,50,1,384]{3,2,1,0:T(1,128)S(1)} %get-tuple-element.28), channel_id=1, source_target_pairs={{0,1},{1,0},{2,3},{3,2},{4,5},{5,4},{6,7},{7,6},{8,9},{9,8},{10,11... | collective-permute-start | bytes 1152008 | tf_op jit(solution)/shard_map/ppermute | solution.py:838
  9.5 0.7 %collective-permute-start.3 = (f32[5,50,1,384]{3,2,1,0:T(1,128)S(1)}, f32[5,50,1,384]{3,2,1,0:T(1,128)S(1)}, u32[]{:S(2)}, u32[]{:S(2)}) collective-permute-start(f32[5,50,1,384]{3,2,1,0:T(1,128)S(1)} %get-tuple-element.29), channel_id=1, source_target_pairs={{1,2},{2,1},{5,6},{6,5},{9,10},{10,9},{13,14},{14,13},{17,18},{18,... | collective-permute-start | bytes 1152008 | tf_op jit(solution)/shard_map/ppermute | solution.py:834
  10.2 0.7 %collective-permute-done.1.refs_2_ = f32[32,16]{1,0:T(8,128)S(1)} collective-permute-done((f32[32,16]{1,0:T(8,128)S(1)}, f32[32,16]{1,0:T(8,128)S(1)}, u32[]{:S(2)}, u32[]{:S(2)}) %collective-permute-start.1) | collective-permute-done | bytes 2080 | tf_op jit(solution)/shard_map/ppermute | solution.py:838
  10.9 4.5 %front.1 = (f32[5,12,56,384]{3,2,1,0:T(8,128)}, bf16[5,128,128]{2,1,0:T(8,128)(2,1)S(1)}, f32[72,128]{1,0:T(8,128)S(1)}, f32[500,128]{1,0:T(8,128)S(1)}, s32[16,16]{1,0:T(8,128)S(1)}) custom-call(s32[1]{0:T(128)} %bitcast.is_child, f32[9000,128]{1,0:T(8,128)} %bitcast.28, s32[12,1,384]{2,1,0:T(1,128)} %bitcast.22, f32[12,1,384]{2,1,0:T(1,128)} %bitcast.13, ...), custom_call_target="tpu_custom_call" | custom-call | flops 10000000000 | bytes 100000000 | tf_op jit(solution)/shard_map/front/pallas_call | solution.py:363
  15.4 0.1 collective-permute-start.4
  15.5 1.9 %collective-permute-start.6 = (f32[500,128]{1,0:T(8,128)S(1)}, f32[500,128]{1,0:T(8,128)S(1)}, u32[]{:S(2)}, u32[]{:S(2)}) collective-permute-start(f32[500,128]{1,0:T(8,128)S(1)} %get-tuple-element.37.in_sent), channel_id=1, source_target_pairs={{0,16},{16,0},{1,17},{17,1},{2,18},{18,2},{3,19},{19,3},{4,20},{20... | collective-permute-start | bytes 768008 | tf_op jit(solution)/shard_map/ppermute | solution.py:838
  17.4 0.0 collective-permute-done.4.arrived.first
  17.4 0.1 repack.1.mine
  17.5 1.3 %collective-permute-start.5 = (f32[72,128]{1,0:T(8,128)S(1)}, f32[72,128]{1,0:T(8,128)S(1)}, u32[]{:S(2)}, u32[]{:S(2)}) collective-permute-start(f32[72,128]{1,0:T(8,128)S(1)} %repack.1.mine), channel_id=1, source_target_pairs={{0,12},{4,8},{8,4},{12,0},{1,13},{5,9},{9,5},{13,1},{2,14},{6,10},... | collective-permute-start | bytes 110600 | tf_op jit(solution)/shard_map/ppermute | solution.py:838
  18.7 0.2 collective-permute-done.2.x_first
  19.0 0.0 collective-permute-done.3.x_second
  19.0 2.9 %base.1 = f32[5,56,256]{2,1,0:T(8,128)S(1)} custom-call(s32[1]{0:T(128)} %bitcast.is_child, s32[1]{0:T(128)S(6)} %copy.15._.nest_x, s32[1]{0:T(128)S(6)} %copy.16.__.nest_y, f32[5,12,56,384]{3,2,1,0:T(8,128)} %get-tuple-element.35.masked_in, bf16[5,128,128]{2,1,0:T(8,128)(2,1)S(1)} %get-tuple-element.32.matrices, f32[12,1,384]{2,1,0:T(1,128)S(1)} %bitcast.14, ...), custom_call_target="tpu_custom_call" | custom-call | flops 10000000000 | bytes 100000000 | tf_op jit(solution)/shard_map/base/pallas_call | solution.py:446
  21.9 0.0 copy-start.4
  21.9 0.0 collective-permute-done.5.second.theirs
  21.9 1.4 %outer.1 = (f32[560,128]{1,0:T(8,128)S(1)}, f32[1800,128]{1,0:T(8,128)S(1)}) custom-call(s32[1]{0:T(128)} %bitcast.is_child, s32[1]{0:T(128)} %bitcast.2.tx.column, s32[1]{0:T(128)} %bitcast.1.ty.row, f32[9000,128]{1,0:T(8,128)} %bitcast.29, bf16[5,128,128]{2,1,0:T(8,128)(2,1)S(1)} %get-tuple-element.32.matrices, f32[5,56,256]{2,1,0:T(8,128)S(1)} %base.1, ...), custom_call_target="tpu_custom_call" | custom-call | tf_op jit(solution)/shard_map/outer/pallas_call | solution.py:591
  23.3 1.5 %collective-permute-start.7 = (f32[560,128]{1,0:T(8,128)S(1)}, f32[560,128]{1,0:T(8,128)S(1)}, u32[]{:S(2)}, u32[]{:S(2)}) collective-permute-start(f32[560,128]{1,0:T(8,128)S(1)} %get-tuple-element.38.out_sent), channel_id=1, source_target_pairs={{0,16},{16,0},{1,17},{17,1},{2,18},{18,2},{3,19},{19,3},{4,20},{20... | collective-permute-start | bytes 860168 | tf_op jit(solution)/shard_map/ppermute | solution.py:838
  24.7 6.2 %tile.1._ = f32[10080,128]{1,0:T(8,128)S(1)} custom-call(s32[1]{0:T(128)} %bitcast.2.tx.column, s32[1]{0:T(128)} %bitcast.1.ty.row, f32[9000,128]{1,0:T(8,128)} %bitcast.30, s32[12,1,384]{2,1,0:T(1,128)S(1)} %bitcast.23, bf16[5,128,128]{2,1,0:T(8,128)(2,1)S(1)} %get-tuple-element.32.matrices, f32[12,1,384]{2,1,0:T(1,128)S(1)} %bitcast.16, ...), custom_call_target="tpu_custom_call" | custom-call | flops 10000000000 | bytes 100000000 | tf_op jit(solution)/shard_map/tile/pallas_call | solution.py:659
  31.0 2.1 %observe.1.tile = f32[10080,128]{1,0:T(8,128)S(1)} custom-call(s32[1]{0:T(128)} %bitcast.1.ty.row, s32[1]{0:T(128)} %bitcast.2.tx.column, s32[1,16]{1,0:T(1,128)S(1)} %bitcast.20, s32[16,16]{1,0:T(8,128)S(1)} %get-tuple-element.26.places, f32[72,128]{1,0:T(8,128)S(1)} %repack.1.mine, ...), custom_call_target="tpu_custom_call", output_to_operand_aliasing={{}: (6, {})} | custom-call | tf_op jit(solution)/shard_map/observe/pallas_call | solution.py:714
  33.1 0.0 collective-permute-done.6.in_arrived
  33.1 2.6 %finish.1 = f32[9000,128]{1,0:T(8,128)} custom-call(s32[1]{0:T(128)} %bitcast.is_child, s32[1]{0:T(128)S(6)} %copy.15._.nest_x, s32[1]{0:T(128)S(6)} %copy.16.__.nest_y, f32[10080,128]{1,0:T(8,128)S(1)} %observe.1.tile, s32[12,1,384]{2,1,0:T(1,128)S(1)} %bitcast.24, f32[500,128]{1,0:T(8,128)S(1)} %collective-permute-done.6.in_arrived, ...), custom_call_target="tpu_custom_call" | custom-call | flops 10000000000 | bytes 100000000 | tf_op jit(solution)/shard_map/finish/pallas_call | solution.py:814
  (13 shorter events, 0.0 us)
Async XLA Ops:
  0.0 6.0 %collective-permute-start = (f32[16,16]{1,0:T(8,128)}, f32[16,16]{1,0:T(8,128)S(1)}, u32[]{:S(2)}, u32[]{:S(2)}) collective-permute-start(f32[16,16]{1,0:T(8,128)} %bitcast.17), channel_id=1, source_target_pairs={{0,1},{1,0},{2,3},{3,2},{4,5},{5,4},{6,7},{7,6},{8,9},{9,8},{10,11... | collective-permute-start | bytes 3080 | tf_op jit(solution)/shard_map/ppermute | solution.py:838
  4.3 1.7 %copy-start.2 = (f32[1,1,16,16]{3,2,1,0:T(8,128)S(1)}, f32[1,1,16,16]{3,2,1,0:T(8,128)}, u32[]{:S(2)}) copy-start(f32[1,1,16,16]{3,2,1,0:T(8,128)} %param.17) | copy-start | bytes 3076
  4.3 6.5 %copy-start.5 = (s32[1,16,16,1]{2,3,1,0:T(1,128)S(1)}, s32[1,16,16,1]{2,3,1,0:T(1,128)}, u32[]{:S(2)}) copy-start(s32[1,16,16,1]{2,3,1,0:T(1,128)} %param.18) | copy-start | bytes 3076
  6.1 4.8 %collective-permute-start.1 = (f32[32,16]{1,0:T(8,128)S(1)}, f32[32,16]{1,0:T(8,128)S(1)}, u32[]{:S(2)}, u32[]{:S(2)}) collective-permute-start(f32[32,16]{1,0:T(8,128)S(1)} %stacked.1), channel_id=1, source_target_pairs={{0,2},{1,3},{2,0},{3,1},{4,6},{5,7},{6,4},{7,5},{8,10},{9,11},{10,... | collective-permute-start | bytes 6152 | tf_op jit(solution)/shard_map/ppermute | solution.py:838
  8.7 10.3 %collective-permute-start.2 = (f32[5,50,1,384]{3,2,1,0:T(1,128)S(1)}, f32[5,50,1,384]{3,2,1,0:T(1,128)S(1)}, u32[]{:S(2)}, u32[]{:S(2)}) collective-permute-start(f32[5,50,1,384]{3,2,1,0:T(1,128)S(1)} %get-tuple-element.28), channel_id=1, source_target_pairs={{0,1},{1,0},{2,3},{3,2},{4,5},{5,4},{6,7},{7,6},{8,9},{9,8},{10,11... | collective-permute-start | bytes 1152008 | tf_op jit(solution)/shard_map/ppermute | solution.py:838
  9.5 9.5 %collective-permute-start.3 = (f32[5,50,1,384]{3,2,1,0:T(1,128)S(1)}, f32[5,50,1,384]{3,2,1,0:T(1,128)S(1)}, u32[]{:S(2)}, u32[]{:S(2)}) collective-permute-start(f32[5,50,1,384]{3,2,1,0:T(1,128)S(1)} %get-tuple-element.29), channel_id=1, source_target_pairs={{1,2},{2,1},{5,6},{6,5},{9,10},{10,9},{13,14},{14,13},{17,18},{18,... | collective-permute-start | bytes 1152008 | tf_op jit(solution)/shard_map/ppermute | solution.py:834
  10.9 8.1 %copy-start = (f32[12,384]{1,0:T(8,128)S(1)}, f32[12,384]{1,0:T(8,128)}, u32[]{:S(2)}) copy-start(f32[12,384]{1,0:T(8,128)} %nudging.5) | copy-start | bytes 55300
  10.9 8.1 %copy-start.1 = (f32[1,12,384]{2,0,1:T(1,128)S(1)}, f32[1,12,384]{2,0,1:T(1,128)}, u32[]{:S(2)}) copy-start(f32[1,12,384]{2,0,1:T(1,128)} %param.12) | copy-start | bytes 55300
  15.4 1.9 %collective-permute-start.4 = (f32[72,128]{1,0:T(8,128)S(1)}, f32[72,128]{1,0:T(8,128)S(1)}, u32[]{:S(2)}, u32[]{:S(2)}) collective-permute-start(f32[72,128]{1,0:T(8,128)S(1)} %get-tuple-element.30.parcel), channel_id=1, source_target_pairs={{0,4},{4,0},{8,12},{12,8},{1,5},{5,1},{9,13},{13,9},{2,6},{6,2},{1... | collective-permute-start | bytes 110600 | tf_op jit(solution)/shard_map/ppermute | solution.py:838
  15.5 17.6 %collective-permute-start.6 = (f32[500,128]{1,0:T(8,128)S(1)}, f32[500,128]{1,0:T(8,128)S(1)}, u32[]{:S(2)}, u32[]{:S(2)}) collective-permute-start(f32[500,128]{1,0:T(8,128)S(1)} %get-tuple-element.37.in_sent), channel_id=1, source_target_pairs={{0,16},{16,0},{1,17},{17,1},{2,18},{18,2},{3,19},{19,3},{4,20},{20... | collective-permute-start | bytes 768008 | tf_op jit(solution)/shard_map/ppermute | solution.py:838
  17.5 4.4 %collective-permute-start.5 = (f32[72,128]{1,0:T(8,128)S(1)}, f32[72,128]{1,0:T(8,128)S(1)}, u32[]{:S(2)}, u32[]{:S(2)}) collective-permute-start(f32[72,128]{1,0:T(8,128)S(1)} %repack.1.mine), channel_id=1, source_target_pairs={{0,12},{4,8},{8,4},{12,0},{1,13},{5,9},{9,5},{13,1},{2,14},{6,10},... | collective-permute-start | bytes 110600 | tf_op jit(solution)/shard_map/ppermute | solution.py:838
  21.9 2.9 %copy-start.4 = (s32[1,12,384]{2,0,1:T(1,128)S(1)}, s32[1,12,384]{2,0,1:T(1,128)}, u32[]{:S(2)}) copy-start(s32[1,12,384]{2,0,1:T(1,128)} %param.11) | copy-start | bytes 55300
  23.3 9.8 %collective-permute-start.7 = (f32[560,128]{1,0:T(8,128)S(1)}, f32[560,128]{1,0:T(8,128)S(1)}, u32[]{:S(2)}, u32[]{:S(2)}) collective-permute-start(f32[560,128]{1,0:T(8,128)S(1)} %get-tuple-element.38.out_sent), channel_id=1, source_target_pairs={{0,16},{16,0},{1,17},{17,1},{2,18},{18,2},{3,19},{19,3},{4,20},{20... | collective-permute-start | bytes 860168 | tf_op jit(solution)/shard_map/ppermute | solution.py:838
  24.7 6.2 %copy-start.3 = (s32[1,16,1]{1,2,0:T(1,128)S(1)}, s32[1,16,1]{1,2,0:T(1,128)}, u32[]{:S(2)}) copy-start(s32[1,16,1]{1,2,0:T(1,128)} %param.19) | copy-start | bytes 196
